TPU v7x, 32 devices: a whole 2x2x4 slice. The times are simulated.
32 devices in a mesh: tok: 8 (over z, y), feat: 4 (over x, core).
Axes of the slice: x: 2, y: 2, z: 4, core: 2. Of those that a mesh axis runs over, the one named last changes fastest.
Arguments:
- inputs: bfloat16 [4096, 960], P('tok', 'feat'), may hold values from -6 to 6
- attn_gain: float32 [960], P('feat'), may hold values from 0.5 to 1.5
- w_query: bfloat16 [960, 960], P('feat', 'tok'), may hold values from -0.1875 to 0.1875
- w_key: bfloat16 [960, 320], P('feat', 'tok'), may hold values from -0.1875 to 0.1875
- value_weight: bfloat16 [960, 320], P('feat', 'tok'), may hold values from -0.1875 to 0.1875
- w_out: bfloat16 [960, 960], P('tok', 'feat'), may hold values from -1 to 1
- ffn_gain: float32 [960], P('feat'), may hold values from 0.5 to 1.5
- w_gate: bfloat16 [960, 2560], P('tok', 'feat'), may hold values from -0.1875 to 0.1875
- w_up: bfloat16 [960, 2560], P('tok', 'feat'), may hold values from -0.1875 to 0.1875
- w_down: bfloat16 [2560, 960], P('feat', 'tok'), may hold values from -0.125 to 0.125
- cot: bfloat16 [4096, 960], P('tok', 'feat'), may hold values from -6 to 6
Outputs:
- block_out: float32 [960, 4096], P('feat', 'tok')
- grad_inputs: float32 [960, 4096], P('feat', 'tok')
- grad_attn_gain: float32 [960], P('feat')
- grad_w_query: float32 [960, 960], P('feat', 'tok')
- grad_w_key: float32 [960, 320], P('feat', 'tok')
- grad_w_value: float32 [960, 320], P('feat', 'tok')
- grad_w_out: float32 [960, 960], P('tok', 'feat')
- grad_ffn_gain: float32 [960], P('feat')
- grad_w_gate: float32 [960, 2560], P('tok', 'feat')
- grad_w_up: float32 [960, 2560], P('tok', 'feat')
- grad_w_down: float32 [2560, 960], P('feat', 'tok')
All inputs are finite; a program needn't handle non-finite values.
Results may differ from a plain program's by a relative error of at most 0.02.
Values may be sent and summed in bfloat16 or wider, within the bound.
A program may use at most 128 MiB of HBM per device.

v0:
```python
import math

import jax
import jax.numpy as jnp
from jax import lax
from jax.sharding import PartitionSpec as P

MODEL_WIDTH = 960
QUERY_HEADS = 15
KEY_HEADS = 5
HEAD_SIZE = 64
SEQ_LEN = 4096
QUERY_PER_KEY = 3


EPS = 1e-05
ROPE_BASE = 10000.0
LARGE_NEGATIVE = -1e30


def shifted(value, axis, steps):
    count = lax.axis_size(axis)
    leading, last = (max(0, -steps), min(count, count - steps))
    return lax.ppermute(value, axis, [(source, source + steps) for source in range(leading, last)])


def rotary_tables(positions):
    half_width = HEAD_SIZE // 2
    inverse_freq = ROPE_BASE ** (-2.0 * jnp.arange(half_width, dtype=jnp.float32) / HEAD_SIZE)
    angles = positions.astype(jnp.float32)[:, None] * inverse_freq[None, :]
    return (jnp.cos(angles)[:, None, :], jnp.sin(angles)[:, None, :])


def apply_rotary(value_matrix, cosine_lookup, sine_lookup, head_count, sign_value):
    shaped = value_matrix.reshape(value_matrix.shape[0], head_count, HEAD_SIZE)
    lead_half = shaped[..., : HEAD_SIZE // 2]
    tail_half = shaped[..., HEAD_SIZE // 2 :]
    out_lead = lead_half * cosine_lookup - sign_value * tail_half * sine_lookup
    out_tail = tail_half * cosine_lookup + sign_value * lead_half * sine_lookup
    return jnp.concatenate([out_lead, out_tail], axis=-1).reshape(
        value_matrix.shape[0], head_count * HEAD_SIZE
    )


def divide_pair(value_matrix):
    high = value_matrix.astype(jnp.bfloat16)
    high = lax.optimization_barrier(high)
    low = (value_matrix - high.astype(jnp.float32)).astype(jnp.bfloat16)
    return high.astype(jnp.float32) + low.astype(jnp.float32)


def on_device(
    inputs, attn_gain, w_query, w_key, value_weight, w_out, ffn_gain, w_gate, w_up, w_down, cot
):
    token_rows = inputs.shape[0]
    feat_count = lax.axis_size("feat")
    tok_count = lax.axis_size("tok")
    local_rows = token_rows // feat_count
    own_width = attn_gain.shape[0]
    span_count = SEQ_LEN // token_rows
    key_value_width = KEY_HEADS * HEAD_SIZE
    score_scale = 1.0 / math.sqrt(HEAD_SIZE)
    tok_index = lax.axis_index("tok")
    feat_index = lax.axis_index("feat")
    block_first = tok_index * token_rows
    seq_start = block_first // SEQ_LEN * SEQ_LEN
    block_depth = (block_first - seq_start) // token_rows
    global_rows = block_first + feat_index * local_rows + jnp.arange(local_rows, dtype=jnp.int32)
    cosine_lookup, sine_lookup = rotary_tables(global_rows - seq_start)
    cosine_block_rows, sine_block_rows = rotary_tables(
        block_first - seq_start + jnp.arange(token_rows, dtype=jnp.int32)
    )
    wq_loc, wk_loc, wv_loc, wo_loc, wg_loc, wu_loc, wd_loc = (
        lax.all_gather(w_query, "tok", axis=1, tiled=True),
        lax.all_gather(w_key, "tok", axis=1, tiled=True),
        lax.all_gather(value_weight, "tok", axis=1, tiled=True),
        lax.all_gather(w_out, "tok", axis=0, tiled=True),
        lax.all_gather(w_gate, "tok", axis=0, tiled=True),
        lax.all_gather(w_up, "tok", axis=0, tiled=True),
        lax.all_gather(w_down, "tok", axis=1, tiled=True),
    )
    qkv_weights = jnp.concatenate([wq_loc, wk_loc, wv_loc], axis=1)
    inputs_wide = inputs.astype(jnp.float32)
    squares_one = lax.psum(jnp.sum(inputs_wide * inputs_wide, axis=1), "feat")
    scale_one = lax.rsqrt(squares_one / MODEL_WIDTH + EPS)[:, None]
    normed_one = (inputs_wide * scale_one * attn_gain[None, :]).astype(jnp.bfloat16)
    picked = normed_one
    local_projection = lax.psum_scatter(
        jnp.dot(picked, qkv_weights, preferred_element_type=jnp.float32),
        "feat",
        scatter_dimension=0,
        tiled=True,
    )
    local_queries = apply_rotary(
        local_projection[:, : QUERY_HEADS * HEAD_SIZE], cosine_lookup, sine_lookup, QUERY_HEADS, 1.0
    ).astype(jnp.bfloat16)
    my_keys = apply_rotary(
        local_projection[:, QUERY_HEADS * HEAD_SIZE : (QUERY_HEADS + KEY_HEADS) * HEAD_SIZE],
        cosine_lookup,
        sine_lookup,
        KEY_HEADS,
        1.0,
    ).astype(jnp.bfloat16)
    local_values = local_projection[:, (QUERY_HEADS + KEY_HEADS) * HEAD_SIZE :].astype(jnp.bfloat16)
    query_head_rows = local_queries.reshape(local_rows, KEY_HEADS, QUERY_PER_KEY, HEAD_SIZE)
    kv_mine = jnp.concatenate([my_keys, local_values], axis=1)
    kv_block = lax.all_gather(kv_mine, "feat", axis=0, tiled=True)

    def attend(carried, key_value_portion, key_first):
        maxima, totals, weighted = carried
        key_row_set = key_value_portion[:, :key_value_width].reshape(
            token_rows, KEY_HEADS, HEAD_SIZE
        )
        value_row_set = (
            key_value_portion[:, key_value_width:]
            .reshape(token_rows, KEY_HEADS, HEAD_SIZE)
            .astype(jnp.float32)
        )
        scores = (
            jnp.einsum(
                "rgcd,ngd->gcrn", query_head_rows, key_row_set, preferred_element_type=jnp.float32
            )
            * score_scale
        )
        key_pos = key_first + jnp.arange(token_rows, dtype=jnp.int32)
        allowed = key_pos[None, :] <= global_rows[:, None]
        masked = jnp.where(allowed, scores, LARGE_NEGATIVE)
        new_max = jnp.maximum(maxima, jnp.max(masked, axis=-1))
        weights = jnp.where(allowed, jnp.exp(masked - new_max[..., None]), 0.0)
        factor = jnp.exp(maxima - new_max)
        return (
            new_max,
            totals * factor + jnp.sum(weights, axis=-1),
            weighted * factor[..., None] + jnp.einsum("gcrn,ngd->gcrd", weights, value_row_set),
        )

    starting_state = (
        jnp.full((KEY_HEADS, QUERY_PER_KEY, local_rows), LARGE_NEGATIVE, jnp.float32),
        jnp.zeros((KEY_HEADS, QUERY_PER_KEY, local_rows), jnp.float32),
        jnp.zeros((KEY_HEADS, QUERY_PER_KEY, local_rows, HEAD_SIZE), jnp.float32),
    )
    carried = attend(starting_state, kv_block, block_first)
    blocks = jnp.concatenate(
        [
            kv_block[None],
            jnp.zeros((span_count - 1, token_rows, 2 * key_value_width), jnp.bfloat16),
        ],
        axis=0,
    )

    def forward_turn(turn_index, loop_state):
        carried_now, key_value_portion, kept_blocks = loop_state
        key_value_portion = shifted(key_value_portion, "tok", 1)
        kept_blocks = lax.dynamic_update_index_in_dim(kept_blocks, key_value_portion, turn_index, 0)
        carried_now = lax.cond(
            turn_index <= block_depth,
            lambda current: attend(
                current, key_value_portion, block_first - turn_index * token_rows
            ),
            lambda current: current,
            carried_now,
        )
        return (carried_now, key_value_portion, kept_blocks)

    carried, last_piece, blocks = lax.fori_loop(
        1, span_count, forward_turn, (carried, kv_block, blocks)
    )
    maxima, totals, weighted = carried
    heads_out = (
        (weighted / totals[..., None])
        .transpose(2, 0, 1, 3)
        .reshape(local_rows, QUERY_HEADS * HEAD_SIZE)
        .astype(jnp.bfloat16)
    )
    logsumexp_totals = (
        (maxima + jnp.log(totals)).transpose(2, 0, 1).reshape(local_rows, QUERY_HEADS)
    )
    heads_all, cot_all = (
        lax.all_gather(heads_out, "feat", axis=0, tiled=True),
        lax.all_gather(cot, "feat", axis=1, tiled=True),
    )
    residual = inputs_wide + jnp.dot(heads_all, wo_loc, preferred_element_type=jnp.float32)
    residual_all, gain_all = (
        lax.all_gather(residual, "feat", axis=1, tiled=True),
        lax.all_gather(ffn_gain, "feat", axis=0, tiled=True),
    )
    scale_two = lax.rsqrt(jnp.mean(residual_all * residual_all, axis=1, keepdims=True) + EPS)
    normed_two = (residual_all * scale_two * gain_all[None, :]).astype(jnp.bfloat16)
    gate_pre = jnp.dot(normed_two, wg_loc, preferred_element_type=jnp.float32)
    up_pre = jnp.dot(normed_two, wu_loc, preferred_element_type=jnp.float32)
    sigmoid_gate = jax.nn.sigmoid(gate_pre)
    hidden = (gate_pre * sigmoid_gate * up_pre).astype(jnp.bfloat16)
    partial_value = jnp.dot(hidden, wd_loc, preferred_element_type=jnp.float32)
    ffn_term = lax.psum_scatter(
        partial_value.astype(jnp.bfloat16), "feat", scatter_dimension=1, tiled=True
    ).astype(jnp.float32)
    block_out = residual + ffn_term
    grad_down = jnp.dot(hidden.T, cot_all, preferred_element_type=jnp.float32)
    d_hidden = jnp.dot(cot_all, wd_loc.T, preferred_element_type=jnp.float32)
    d_gate = (d_hidden * up_pre * sigmoid_gate * (1.0 + gate_pre * (1.0 - sigmoid_gate))).astype(
        jnp.bfloat16
    )
    d_up = (d_hidden * gate_pre * sigmoid_gate).astype(jnp.bfloat16)
    grad_gate = jnp.dot(normed_two.T, d_gate, preferred_element_type=jnp.float32)
    grad_up = jnp.dot(normed_two.T, d_up, preferred_element_type=jnp.float32)
    back_two = jnp.dot(d_gate, wg_loc.T, preferred_element_type=jnp.float32) + jnp.dot(
        d_up, wu_loc.T, preferred_element_type=jnp.float32
    )
    summed_two = lax.psum(back_two.astype(jnp.bfloat16), "feat").astype(jnp.float32)
    stat_two = jnp.sum(summed_two * gain_all[None, :] * residual_all, axis=1, keepdims=True)
    d_norm_two = lax.dynamic_slice_in_dim(summed_two, feat_index * own_width, own_width, 1)
    d_mid = (
        cot.astype(jnp.float32)
        + scale_two * ffn_gain[None, :] * d_norm_two
        - residual * scale_two**3 * stat_two / MODEL_WIDTH
    )
    gain_two_term = jnp.sum(d_norm_two * residual * scale_two, axis=0)
    d_attn = d_mid.astype(jnp.bfloat16)
    grad_out = jnp.dot(heads_all.T, d_attn, preferred_element_type=jnp.float32)
    picked = d_attn
    head_gradient = lax.psum_scatter(
        jnp.dot(picked, wo_loc.T, preferred_element_type=jnp.float32).astype(jnp.bfloat16),
        "feat",
        scatter_dimension=0,
        tiled=True,
    )
    difference_rows = jnp.sum(
        (head_gradient.astype(jnp.float32) * heads_out.astype(jnp.float32)).reshape(
            local_rows, QUERY_HEADS, HEAD_SIZE
        ),
        axis=-1,
    )
    local_logsumexp = (
        divide_pair(logsumexp_totals)
        .reshape(local_rows, KEY_HEADS, QUERY_PER_KEY)
        .transpose(1, 2, 0)
    )
    local_difference = (
        divide_pair(difference_rows)
        .reshape(local_rows, KEY_HEADS, QUERY_PER_KEY)
        .transpose(1, 2, 0)
    )
    head_gradient_rows = head_gradient.reshape(local_rows, KEY_HEADS, QUERY_PER_KEY, HEAD_SIZE)
    dhead_wide = head_gradient_rows.astype(jnp.float32)
    query_wide = query_head_rows.astype(jnp.float32)

    def backprop(loop_state, key_value_portion, key_first):
        query_gradient_sum, gradient_totals = loop_state
        key_row_set = key_value_portion[:, :key_value_width].reshape(
            token_rows, KEY_HEADS, HEAD_SIZE
        )
        value_row_set = key_value_portion[:, key_value_width:].reshape(
            token_rows, KEY_HEADS, HEAD_SIZE
        )
        scores = (
            jnp.einsum(
                "rgcd,ngd->gcrn", query_head_rows, key_row_set, preferred_element_type=jnp.float32
            )
            * score_scale
        )
        key_pos = key_first + jnp.arange(token_rows, dtype=jnp.int32)
        allowed = key_pos[None, :] <= global_rows[:, None]
        masked = jnp.where(allowed, scores, LARGE_NEGATIVE)
        probability = jnp.where(allowed, jnp.exp(masked - local_logsumexp[..., None]), 0.0)
        d_probs = jnp.einsum(
            "rgcd,ngd->gcrn", head_gradient_rows, value_row_set, preferred_element_type=jnp.float32
        )
        d_scores = probability * (d_probs - local_difference[..., None])
        query_gradient_sum = (
            query_gradient_sum
            + jnp.einsum("gcrn,ngd->gcrd", d_scores, key_row_set.astype(jnp.float32)) * score_scale
        )
        key_part = jnp.einsum("gcrn,rgcd->ngd", d_scores, query_wide) * score_scale
        value_part = jnp.einsum("gcrn,rgcd->ngd", probability, dhead_wide)
        gradient_totals = gradient_totals + jnp.concatenate(
            [
                key_part.reshape(token_rows, key_value_width),
                value_part.reshape(token_rows, key_value_width),
            ],
            axis=1,
        )
        return (query_gradient_sum, gradient_totals)

    def backward_turn(turn_index, loop_state):
        back_index = span_count - 1 - turn_index
        key_value_portion = lax.dynamic_index_in_dim(blocks, back_index, 0, keepdims=False)
        loop_state = lax.cond(
            back_index <= block_depth,
            lambda current: backprop(
                current, key_value_portion, block_first - back_index * token_rows
            ),
            lambda current: current,
            loop_state,
        )
        query_gradient_sum, gradient_totals = loop_state
        gradient_totals = shifted(gradient_totals.astype(jnp.bfloat16), "tok", -1).astype(
            gradient_totals.dtype
        )
        return (query_gradient_sum, gradient_totals)

    grads_init = (
        jnp.zeros((KEY_HEADS, QUERY_PER_KEY, local_rows, HEAD_SIZE), jnp.float32),
        jnp.zeros((token_rows, 2 * key_value_width), jnp.float32),
    )
    loop_state = lax.fori_loop(0, span_count - 1, backward_turn, grads_init)
    query_gradient_sum, gradient_totals = backprop(loop_state, kv_block, block_first)
    key_gradient_block = apply_rotary(
        gradient_totals[:, :key_value_width], cosine_block_rows, sine_block_rows, KEY_HEADS, -1.0
    )
    query_grad_own = apply_rotary(
        query_gradient_sum.transpose(2, 0, 1, 3).reshape(local_rows, QUERY_HEADS * HEAD_SIZE),
        cosine_lookup,
        sine_lookup,
        QUERY_HEADS,
        -1.0,
    )
    query_grad_block = lax.dynamic_update_slice_in_dim(
        jnp.zeros((token_rows, QUERY_HEADS * HEAD_SIZE), jnp.float32),
        query_grad_own,
        feat_index * local_rows,
        0,
    )
    d_qkv_all = lax.psum(
        jnp.concatenate(
            [query_grad_block, key_gradient_block, gradient_totals[:, key_value_width:]], axis=1
        ).astype(jnp.bfloat16),
        "feat",
    )
    projection_gradient = jnp.dot(normed_one.T, d_qkv_all, preferred_element_type=jnp.float32)
    back_one = jnp.dot(d_qkv_all, qkv_weights.T, preferred_element_type=jnp.float32)
    stat_one = lax.psum(jnp.sum(back_one * attn_gain[None, :] * inputs_wide, axis=1), "feat")[
        :, None
    ]
    grad_inputs = (
        d_mid
        + scale_one * attn_gain[None, :] * back_one
        - inputs_wide * scale_one**3 * stat_one / MODEL_WIDTH
    )
    gain_one_term = jnp.sum(back_one * inputs_wide * scale_one, axis=0)
    gains_term = jnp.broadcast_to(
        jnp.stack([gain_one_term, gain_two_term])[None], (tok_count, 2, own_width)
    )
    grad_query, grad_key, grad_value, grad_wout, grad_wgate, grad_wup, grad_wdown, gains_sum = (
        lax.psum_scatter(
            projection_gradient[:, : QUERY_HEADS * HEAD_SIZE],
            "tok",
            scatter_dimension=1,
            tiled=True,
        ),
        lax.psum_scatter(
            projection_gradient[:, QUERY_HEADS * HEAD_SIZE : (QUERY_HEADS + KEY_HEADS) * HEAD_SIZE],
            "tok",
            scatter_dimension=1,
            tiled=True,
        ),
        lax.psum_scatter(
            projection_gradient[:, (QUERY_HEADS + KEY_HEADS) * HEAD_SIZE :],
            "tok",
            scatter_dimension=1,
            tiled=True,
        ),
        lax.psum_scatter(grad_out, "tok", scatter_dimension=0, tiled=True),
        lax.psum_scatter(grad_gate, "tok", scatter_dimension=0, tiled=True),
        lax.psum_scatter(grad_up, "tok", scatter_dimension=0, tiled=True),
        lax.psum_scatter(grad_down, "tok", scatter_dimension=1, tiled=True),
        lax.psum_scatter(gains_term, "tok", scatter_dimension=0, tiled=True),
    )
    return (
        block_out.T,
        grad_inputs.T,
        gains_sum[0, 0],
        grad_query,
        grad_key,
        grad_value,
        grad_wout,
        gains_sum[0, 1],
        grad_wgate,
        grad_wup,
        grad_wdown,
    )


def solution(mesh):
    return jax.shard_map(
        on_device,
        mesh=mesh,
        in_specs=(
            P("tok", "feat"),
            P("feat"),
            P("feat", "tok"),
            P("feat", "tok"),
            P("feat", "tok"),
            P("tok", "feat"),
            P("feat"),
            P("tok", "feat"),
            P("tok", "feat"),
            P("feat", "tok"),
            P("tok", "feat"),
        ),
        out_specs=(
            P("feat", "tok"),
            P("feat", "tok"),
            P("feat"),
            P("feat", "tok"),
            P("feat", "tok"),
            P("feat", "tok"),
            P("tok", "feat"),
            P("feat"),
            P("tok", "feat"),
            P("tok", "feat"),
            P("feat", "tok"),
        ),
        check_vma=False,
    )
```

profile of v0, /device:TPU:0, one launch (start us, length us, event | category | flops | bytes accessed | tf_op | source)
XLA Modules:
  0.0 1323.2 jit_solution(5152130786004314782)
XLA Ops:
  11.1 9.0 all-reduce.6
  21.7 31.8 %all_gather.36 = bf16[240,960]{0,1:T(8,128)(2,1)S(1)} all-gather(bf16[240,120]{0,1:T(8,128)(2,1)S(1)} %copy.38), channel_id=1, replica_groups=mesh['tok'=8,'feat'=4] {'tok'}, dimensions={1}, use_global_device_ids=true | all-gather | bytes 518400 | tf_op jit(solution)/shard_map/all_gather | solution.py:74
  53.6 30.6 %all_gather.37 = bf16[240,320]{0,1:T(8,128)(2,1)S(1)} all-gather(bf16[240,40]{0,1:T(8,128)(2,1)S(1)} %copy-done.41), channel_id=1, replica_groups=mesh['tok'=8,'feat'=4] {'tok'}, dimensions={1}, use_global_device_ids=true | all-gather | bytes 172800 | tf_op jit(solution)/shard_map/all_gather | solution.py:75
  84.1 30.6 %all_gather.38 = bf16[240,320]{0,1:T(8,128)(2,1)S(1)} all-gather(bf16[240,40]{0,1:T(8,128)(2,1)S(1)} %copy-done.42), channel_id=1, replica_groups=mesh['tok'=8,'feat'=4] {'tok'}, dimensions={1}, use_global_device_ids=true | all-gather | bytes 172800 | tf_op jit(solution)/shard_map/all_gather | solution.py:76
  115.7 2.4 fusion.60
  118.9 31.1 %all_gather.41 = bf16[960,240]{1,0:T(8,128)(2,1)S(1)} all-gather(bf16[120,240]{1,0:T(8,128)(2,1)S(1)} %copy-done.40), channel_id=1, replica_groups=mesh['tok'=8,'feat'=4] {'tok'}, dimensions={0}, use_global_device_ids=true | all-gather | bytes 518400 | tf_op jit(solution)/shard_map/all_gather | solution.py:77
  150.9 6.2 reduce-scatter.25.cloned.1.call-done
  158.5 7.5 all_gather.39
  169.6 2.8 concatenate.40
  172.3 128.9 %while.42 = (s32[]{:T(128)}, f32[5,3,128]{2,1,0:T(4,128)S(1)}, f32[5,3,128]{2,1,0:T(4,128)S(1)}, f32[5,3,128,64]{2,3,1,0:T(8,128)S(1)}, bf16[512,640]{0,1:T(8,12...) while((s32[]{:T(128)}, f32[5,3,128]{2,1,0:T(4,128)S(1)}, ...), condition=%wide.region_10.11_spmd.clone, body=%wide.region_5.10_spmd.clone.sunk | while | flops 263770496 | bytes 20625792 | solution.py:165
  172.3 3.4 collective-permute-start
  175.7 14.4 %collective-permute-done = bf16[512,640]{0,1:T(8,128)(2,1)S(1)} collective-permute-done((bf16[512,640]{0,1:T(8,128)(2,1)S(1)}, bf16[512,640]{0,1:T(8,128)(2,1)S(1)}, u32[]{:S(2)}, u32[]{:S(2)}) %collective-permute-start) | collective-permute-done | bytes 655392 | tf_op jit(solution)/shard_map/while/body/eval_jaxpr/ppermute | solution.py:24
  191.1 7.5 collective-permute-start
  198.7 13.6 %collective-permute-done = bf16[512,640]{0,1:T(8,128)(2,1)S(1)} collective-permute-done((bf16[512,640]{0,1:T(8,128)(2,1)S(1)}, bf16[512,640]{0,1:T(8,128)(2,1)S(1)}, u32[]{:S(2)}, u32[]{:S(2)}) %collective-permute-start) | collective-permute-done | bytes 655392 | tf_op jit(solution)/shard_map/while/body/eval_jaxpr/ppermute | solution.py:24
  213.3 4.4 collective-permute-start
  217.7 12.7 collective-permute-done
  231.4 8.3 collective-permute-start
  239.7 11.8 collective-permute-done
  252.5 5.3 collective-permute-start
  257.8 10.9 collective-permute-done
  269.6 5.3 collective-permute-start
  274.9 9.9 collective-permute-done
  285.9 5.3 collective-permute-start
  291.2 9.0 collective-permute-done
  301.3 9.3 all_gather.40
  314.7 10.4 all_gather.47
  325.2 27.6 %all-gather.5.cloned.1.call-done = f32[512,960]{0,1:T(8,128)} async-done(((f32[512,240]{0,1:T(8,128)}), f32[512,960]{0,1:T(8,128)}) %all-gather.5.cloned.1.call-update) | async-done | bytes 1966096 | tf_op jit(solution)/shard_map/all_gather | solution.py:184
  352.7 1.9 multiply_reduce_fusion.1
  356.2 41.5 %all-gather.7.cloned.1.call-done = bf16[960,640]{1,0:T(8,128)(2,1)} async-done(((bf16[120,640]{1,0:T(8,128)(2,1)}), bf16[960,640]{1,0:T(8,128)(2,1)}) %all-gather.7.cloned.1.call-update) | async-done | bytes 1228816 | tf_op jit(solution)/shard_map/all_gather | solution.py:78
  397.7 3.4 fusion.74
  401.0 39.2 %all-gather.9.cloned.1.call-done = bf16[960,640]{1,0:T(8,128)(2,1)} async-done(((bf16[120,640]{1,0:T(8,128)(2,1)}), bf16[960,640]{1,0:T(8,128)(2,1)}) %all-gather.9.cloned.1.call-update) | async-done | bytes 1228816 | tf_op jit(solution)/shard_map/all_gather | solution.py:79
  440.2 3.4 fusion.75
  443.6 39.1 %all-gather.11.cloned.1.call-done = bf16[640,960]{0,1:T(8,128)(2,1)} async-done(((bf16[640,120]{0,1:T(8,128)(2,1)}), bf16[640,960]{0,1:T(8,128)(2,1)}) %all-gather.11.cloned.1.call-update) | async-done | bytes 1228816 | tf_op jit(solution)/shard_map/all_gather | solution.py:80
  482.7 3.9 multiply_convert_fusion.1
  488.6 1.9 add_convert_fusion
  490.6 3.2 convolution_convert_fusion.1
  493.9 31.2 %all-reduce.10.cloned.1.call-done = bf16[512,960]{0,1:T(8,128)(2,1)} async-done(((bf16[512,960]{0,1:T(8,128)(2,1)}), bf16[512,960]{0,1:T(8,128)(2,1)}) %all-reduce.10.cloned.1.call-update) | async-done | bytes 983056 | tf_op jit(solution)/shard_map/psum | solution.py:209
  525.1 2.9 convert_element_type.171
  528.3 24.1 %reduce-scatter.27.cloned.1.call-done = bf16[512,240]{0,1:T(8,128)(2,1)} async-done(((bf16[512,960]{0,1:T(8,128)(2,1)}), bf16[512,240]{0,1:T(8,128)(2,1)}) %reduce-scatter.27.cloned.1.call-update) | async-done | bytes 245776 | tf_op jit(solution)/shard_map/reduce_scatter | solution.py:194
  552.5 2.6 multiply_reduce_fusion.2
  559.0 23.7 %reduce-scatter.31.cloned.1.call-done = bf16[128,960]{1,0:T(8,128)(2,1)} async-done(((bf16[512,960]{1,0:T(8,128)(2,1)}), bf16[128,960]{1,0:T(8,128)(2,1)}) %reduce-scatter.31.cloned.1.call-update) | async-done | bytes 245776
  584.0 3.9 fusion.35
  590.8 190.9 %while.43 = (s32[]{:T(128)}, f32[5,3,128,64]{2,3,1,0:T(8,128)S(1)}, f32[512,640]{0,1:T(8,128)S(1)}, s32[]{:T(128)}, s32[]{:T(128)}, /*index=5*/bf16[8,512,640]{1...) while((s32[]{:T(128)}, f32[5,3,128,64]{2,3,1,0:T(8,128)S(1)}, ...), condition=%wide.region_20.21_spmd.clone, body=%wide.region_17.20_spmd.clone.sunk | while | flops 642073216 | bytes 55604240 | solution.py:305
  592.4 17.1 %collective-permute-done.1 = bf16[512,640]{0,1:T(8,128)(2,1)S(1)} collective-permute-done((bf16[512,640]{0,1:T(8,128)(2,1)S(1)}, bf16[512,640]{0,1:T(8,128)(2,1)S(1)}, u32[]{:S(2)}, u32[]{:S(2)}) %collective-permute-start.1) | collective-permute-done | bytes 655392 | tf_op jit(solution)/shard_map/while/body/eval_jaxpr/ppermute | solution.py:24
  611.2 16.8 %collective-permute-done.1 = bf16[512,640]{0,1:T(8,128)(2,1)S(1)} collective-permute-done((bf16[512,640]{0,1:T(8,128)(2,1)S(1)}, bf16[512,640]{0,1:T(8,128)(2,1)S(1)}, u32[]{:S(2)}, u32[]{:S(2)}) %collective-permute-start.1) | collective-permute-done | bytes 655392 | tf_op jit(solution)/shard_map/while/body/eval_jaxpr/ppermute | solution.py:24
  629.8 16.2 %collective-permute-done.1 = bf16[512,640]{0,1:T(8,128)(2,1)S(1)} collective-permute-done((bf16[512,640]{0,1:T(8,128)(2,1)S(1)}, bf16[512,640]{0,1:T(8,128)(2,1)S(1)}, u32[]{:S(2)}, u32[]{:S(2)}) %collective-permute-start.1) | collective-permute-done | bytes 655392 | tf_op jit(solution)/shard_map/while/body/eval_jaxpr/ppermute | solution.py:24
  647.7 15.3 %collective-permute-done.1 = bf16[512,640]{0,1:T(8,128)(2,1)S(1)} collective-permute-done((bf16[512,640]{0,1:T(8,128)(2,1)S(1)}, bf16[512,640]{0,1:T(8,128)(2,1)S(1)}, u32[]{:S(2)}, u32[]{:S(2)}) %collective-permute-start.1) | collective-permute-done | bytes 655392 | tf_op jit(solution)/shard_map/while/body/eval_jaxpr/ppermute | solution.py:24
  664.7 14.3 %collective-permute-done.1 = bf16[512,640]{0,1:T(8,128)(2,1)S(1)} collective-permute-done((bf16[512,640]{0,1:T(8,128)(2,1)S(1)}, bf16[512,640]{0,1:T(8,128)(2,1)S(1)}, u32[]{:S(2)}, u32[]{:S(2)}) %collective-permute-start.1) | collective-permute-done | bytes 655392 | tf_op jit(solution)/shard_map/while/body/eval_jaxpr/ppermute | solution.py:24
  680.8 13.4 %collective-permute-done.1 = bf16[512,640]{0,1:T(8,128)(2,1)S(1)} collective-permute-done((bf16[512,640]{0,1:T(8,128)(2,1)S(1)}, bf16[512,640]{0,1:T(8,128)(2,1)S(1)}, u32[]{:S(2)}, u32[]{:S(2)}) %collective-permute-start.1) | collective-permute-done | bytes 655392 | tf_op jit(solution)/shard_map/while/body/eval_jaxpr/ppermute | solution.py:24
  696.0 85.5 %collective-permute-done.1 = bf16[512,640]{0,1:T(8,128)(2,1)S(1)} collective-permute-done((bf16[512,640]{0,1:T(8,128)(2,1)S(1)}, bf16[512,640]{0,1:T(8,128)(2,1)S(1)}, u32[]{:S(2)}, u32[]{:S(2)}) %collective-permute-start.1) | collective-permute-done | bytes 655392 | tf_op jit(solution)/shard_map/while/body/eval_jaxpr/ppermute | solution.py:24
  788.1 46.1 %all-reduce.12.cloned.1.call-done = bf16[512,1600]{0,1:T(8,128)(2,1)} async-done(((bf16[512,1600]{0,1:T(8,128)(2,1)}), bf16[512,1600]{0,1:T(8,128)(2,1)}) %all-reduce.12.cloned.1.call-update) | async-done | bytes 1638416 | tf_op jit(solution)/shard_map/psum | solution.py:323
  834.2 2.1 fusion.58
  840.6 2.4 fusion.77
  844.1 2.5 fusion.78
  848.0 2.3 fusion.79
  854.2 2.2 fusion.54
  856.5 6.1 psum.31
  862.7 37.4 %all-reduce.2 = f32[8,2,240]{2,1,0:T(2,128)S(1)} all-reduce(f32[8,2,240]{2,1,0:T(2,128)S(1)} %broadcast_in_dim.118), channel_id=5, replica_groups=mesh['tok'=8,'feat'=4] {'tok'}, use_global_device_ids=true, to_apply=%region_26.27.clone | all-reduce | flops 3840 | bytes 30720
  904.2 64.6 %reduce-scatter.29.cloned.1.call-done = f32[120,240]{1,0:T(8,128)} async-done(((f32[960,240]{1,0:T(8,128)}), f32[120,240]{1,0:T(8,128)}) %reduce-scatter.29.cloned.1.call-update) | async-done | bytes 115216 | tf_op jit(solution)/shard_map/reduce_scatter | solution.py:362
  968.7 73.2 %reduce-scatter.39.cloned.1.call-done = f32[120,640]{1,0:T(8,128)} async-done(((f32[960,640]{1,0:T(8,128)}), f32[120,640]{1,0:T(8,128)}) %reduce-scatter.39.cloned.1.call-update) | async-done | bytes 307216
  1041.9 73.2 %reduce-scatter.41.cloned.1.call-done = f32[120,640]{1,0:T(8,128)} async-done(((f32[960,640]{1,0:T(8,128)}), f32[120,640]{1,0:T(8,128)}) %reduce-scatter.41.cloned.1.call-update) | async-done | bytes 307216
  1115.1 73.0 %reduce-scatter.43.cloned.1.call-done = f32[640,120]{0,1:T(8,128)} async-done(((f32[640,960]{0,1:T(8,128)}), f32[640,120]{0,1:T(8,128)}) %reduce-scatter.43.cloned.1.call-update) | async-done | bytes 307216
  1188.1 64.2 %reduce-scatter.35.cloned.1.call-done = f32[40,240]{1,0:T(8,128)} async-done(((f32[320,240]{1,0:T(8,128)}), f32[40,240]{1,0:T(8,128)}) %reduce-scatter.35.cloned.1.call-update) | async-done | bytes 38416
  1252.2 64.4 %reduce-scatter.37.cloned.1.call-done = f32[40,240]{1,0:T(8,128)} async-done(((f32[320,240]{1,0:T(8,128)}), f32[40,240]{1,0:T(8,128)}) %reduce-scatter.37.cloned.1.call-update) | async-done | bytes 38416
  (285 shorter events, 67.7 us)
Async XLA Ops:
  7.2 108.5 %copy-start.14 = (bf16[512,240]{0,1:T(8,128)(2,1)S(1)}, bf16[512,240]{0,1:T(8,128)(2,1)}, u32[]{:S(2)}) copy-start(bf16[512,240]{0,1:T(8,128)(2,1)} %param.19) | copy-start | bytes 737284
  7.2 46.4 %copy-start.41 = (bf16[240,40]{0,1:T(8,128)(2,1)S(1)}, bf16[240,40]{0,1:T(8,128)(2,1)}, u32[]{:S(2)}) copy-start(bf16[240,40]{0,1:T(8,128)(2,1)} %param.22) | copy-start | bytes 57604
  7.2 76.9 %copy-start.42 = (bf16[240,40]{0,1:T(8,128)(2,1)S(1)}, bf16[240,40]{0,1:T(8,128)(2,1)}, u32[]{:S(2)}) copy-start(bf16[240,40]{0,1:T(8,128)(2,1)} %param.23) | copy-start | bytes 57604
  7.2 108.5 %copy-start.44 = (f32[240]{0:T(256)S(1)}, f32[240]{0:T(256)}, u32[]{:S(2)}) copy-start(f32[240]{0:T(256)} %param.20) | copy-start | bytes 2884
  7.2 149.9 %reduce-scatter.25.cloned.1.call-start = ((), (), s32[]{:S(2)}) async-start(), calls=%async_computation.10 | async-start | bytes 4096000 | tf_op jit(solution)/shard_map/reduce_scatter | solution.py:88
  118.1 234.7 %all-gather.5.cloned.1.call-start = ((), (), s32[]{:S(2)}) async-start(), calls=%async_computation.11 | async-start | bytes 2457600 | tf_op jit(solution)/shard_map/all_gather | solution.py:184
  118.2 47.8 %copy-start.50 = (f32[32]{0:T(128)}, f32[32]{0:T(128)S(1)}, u32[]{:S(2)}) copy-start(f32[32]{0:T(128)S(1)} %multiply_power_fusion) | copy-start | bytes 388
  150.0 160.6 %copy-start.17 = (bf16[960,240]{1,0:T(8,128)(2,1)}, bf16[960,240]{1,0:T(8,128)(2,1)S(1)}, u32[]{:S(2)}) copy-start(bf16[960,240]{1,0:T(8,128)(2,1)S(1)} %all_gather.41) | copy-start | bytes 1382404
  166.9 1.9 copy-start.1
  172.3 17.9 %collective-permute-start = (bf16[512,640]{0,1:T(8,128)(2,1)S(1)}, bf16[512,640]{0,1:T(8,128)(2,1)S(1)}, u32[]{:S(2)}, u32[]{:S(2)}) collective-permute-start(bf16[512,640]{0,1:T(8,128)(2,1)S(1)} %get-tuple-element.1112), channel_id=1, source_target_pairs={{0,4},{4,8},{8,12},{12,16},{16,20},{20,24},{24,28},{1,5},{5,9},{9,... | collective-permute-start | bytes 1966088 | tf_op jit(solution)/shard_map/while/body/eval_jaxpr/ppermute | solution.py:24
  191.1 21.2 %collective-permute-start = (bf16[512,640]{0,1:T(8,128)(2,1)S(1)}, bf16[512,640]{0,1:T(8,128)(2,1)S(1)}, u32[]{:S(2)}, u32[]{:S(2)}) collective-permute-start(bf16[512,640]{0,1:T(8,128)(2,1)S(1)} %get-tuple-element.1112), channel_id=1, source_target_pairs={{0,4},{4,8},{8,12},{12,16},{16,20},{20,24},{24,28},{1,5},{5,9},{9,... | collective-permute-start | bytes 1966088 | tf_op jit(solution)/shard_map/while/body/eval_jaxpr/ppermute | solution.py:24
  213.3 17.2 %collective-permute-start = (bf16[512,640]{0,1:T(8,128)(2,1)S(1)}, bf16[512,640]{0,1:T(8,128)(2,1)S(1)}, u32[]{:S(2)}, u32[]{:S(2)}) collective-permute-start(bf16[512,640]{0,1:T(8,128)(2,1)S(1)} %get-tuple-element.1112), channel_id=1, source_target_pairs={{0,4},{4,8},{8,12},{12,16},{16,20},{20,24},{24,28},{1,5},{5,9},{9,... | collective-permute-start | bytes 1966088 | tf_op jit(solution)/shard_map/while/body/eval_jaxpr/ppermute | solution.py:24
  231.4 20.1 %collective-permute-start = (bf16[512,640]{0,1:T(8,128)(2,1)S(1)}, bf16[512,640]{0,1:T(8,128)(2,1)S(1)}, u32[]{:S(2)}, u32[]{:S(2)}) collective-permute-start(bf16[512,640]{0,1:T(8,128)(2,1)S(1)} %get-tuple-element.1112), channel_id=1, source_target_pairs={{0,4},{4,8},{8,12},{12,16},{16,20},{20,24},{24,28},{1,5},{5,9},{9,... | collective-permute-start | bytes 1966088 | tf_op jit(solution)/shard_map/while/body/eval_jaxpr/ppermute | solution.py:24
  252.5 16.2 %collective-permute-start = (bf16[512,640]{0,1:T(8,128)(2,1)S(1)}, bf16[512,640]{0,1:T(8,128)(2,1)S(1)}, u32[]{:S(2)}, u32[]{:S(2)}) collective-permute-start(bf16[512,640]{0,1:T(8,128)(2,1)S(1)} %get-tuple-element.1112), channel_id=1, source_target_pairs={{0,4},{4,8},{8,12},{12,16},{16,20},{20,24},{24,28},{1,5},{5,9},{9,... | collective-permute-start | bytes 1966088 | tf_op jit(solution)/shard_map/while/body/eval_jaxpr/ppermute | solution.py:24
  269.6 15.3 %collective-permute-start = (bf16[512,640]{0,1:T(8,128)(2,1)S(1)}, bf16[512,640]{0,1:T(8,128)(2,1)S(1)}, u32[]{:S(2)}, u32[]{:S(2)}) collective-permute-start(bf16[512,640]{0,1:T(8,128)(2,1)S(1)} %get-tuple-element.1112), channel_id=1, source_target_pairs={{0,4},{4,8},{8,12},{12,16},{16,20},{20,24},{24,28},{1,5},{5,9},{9,... | collective-permute-start | bytes 1966088 | tf_op jit(solution)/shard_map/while/body/eval_jaxpr/ppermute | solution.py:24
  285.9 14.4 %collective-permute-start = (bf16[512,640]{0,1:T(8,128)(2,1)S(1)}, bf16[512,640]{0,1:T(8,128)(2,1)S(1)}, u32[]{:S(2)}, u32[]{:S(2)}) collective-permute-start(bf16[512,640]{0,1:T(8,128)(2,1)S(1)} %get-tuple-element.1112), channel_id=1, source_target_pairs={{0,4},{4,8},{8,12},{12,16},{16,20},{20,24},{24,28},{1,5},{5,9},{9,... | collective-permute-start | bytes 1966088 | tf_op jit(solution)/shard_map/while/body/eval_jaxpr/ppermute | solution.py:24
  301.3 13.5 %copy-start.26 = (bf16[512,240]{0,1:T(8,128)(2,1)S(1)}, bf16[512,240]{0,1:T(8,128)(2,1)}, u32[]{:S(2)}) copy-start(bf16[512,240]{0,1:T(8,128)(2,1)} %param.29) | copy-start | bytes 737284
  312.8 84.9 %all-gather.7.cloned.1.call-start = ((), (), s32[]{:S(2)}) async-start(), calls=%async_computation.12 | async-start | bytes 1382400 | tf_op jit(solution)/shard_map/all_gather | solution.py:78
  313.5 126.7 %all-gather.9.cloned.1.call-start = ((), (), s32[]{:S(2)}) async-start(), calls=%async_computation.13 | async-start | bytes 1382400 | tf_op jit(solution)/shard_map/all_gather | solution.py:79
  314.1 168.6 %all-gather.11.cloned.1.call-start = ((), (), s32[]{:S(2)}) async-start(), calls=%async_computation.14 | async-start | bytes 1382400 | tf_op jit(solution)/shard_map/all_gather | solution.py:80
  314.7 210.4 %all-reduce.10.cloned.1.call-start = ((), (), s32[]{:S(2)}) async-start(), calls=%async_computation.16 | async-start | bytes 1966080 | tf_op jit(solution)/shard_map/psum | solution.py:209
  352.7 2.5 copy-start.5
  356.1 84.1 %copy-start.3 = (bf16[512,960]{0,1:T(8,128)(2,1)}, bf16[512,960]{0,1:T(8,128)(2,1)S(1)}, u32[]{:S(2)}) copy-start(bf16[512,960]{0,1:T(8,128)(2,1)S(1)} %multiply_convert_fusion) | copy-start | bytes 2949124
  482.7 3.9 copy-start.52
  486.6 4.0 copy-start.29
  486.7 2.0 copy-start.53
  490.6 61.9 %reduce-scatter.27.cloned.1.call-start = ((), (), s32[]{:S(2)}) async-start(), calls=%async_computation.15 | async-start | bytes 1228800 | tf_op jit(solution)/shard_map/reduce_scatter | solution.py:194
  493.8 34.1 %copy-start.43 = (f32[960]{0:T(1024)S(1)}, f32[960]{0:T(1024)}, u32[]{:S(2)}) copy-start(f32[960]{0:T(1024)} %get-tuple-element.892) | copy-start | bytes 11524
  493.9 88.8 %reduce-scatter.31.cloned.1.call-start = ((), (), s32[]{:S(2)}) async-start(), calls=%async_computation.19 | async-start | bytes 1310720
  525.1 2.9 copy-start.19
  528.0 24.5 %copy-start.16 = (f32[512,240]{0,1:T(8,128)S(1)}, f32[512,240]{0,1:T(8,128)}, u32[]{:S(2)}) copy-start(f32[512,240]{0,1:T(8,128)} %convolution_add_fusion) | copy-start | bytes 1474564
  528.0 24.5 %copy-start.27 = (bf16[512,240]{0,1:T(8,128)(2,1)S(1)}, bf16[512,240]{0,1:T(8,128)(2,1)}, u32[]{:S(2)}) copy-start(bf16[512,240]{0,1:T(8,128)(2,1)} %param.29) | copy-start | bytes 737284
  528.0 24.5 %copy-start.47 = (f32[512]{0:T(512)S(1)}, f32[512]{0:T(512)}, u32[]{:S(2)}) copy-start(f32[512]{0:T(512)} %get-tuple-element.927) | copy-start | bytes 6148
  528.0 24.5 %copy-start.48 = (f32[240]{0:T(256)S(1)}, f32[240]{0:T(256)}, u32[]{:S(2)}) copy-start(f32[240]{0:T(256)} %param.25) | copy-start | bytes 2884
  528.3 27.5 %copy-start.18 = (bf16[960,240]{1,0:T(8,128)(2,1)S(1)}, bf16[960,240]{1,0:T(8,128)(2,1)}, u32[]{:S(2)}) copy-start(bf16[960,240]{1,0:T(8,128)(2,1)} %copy-done.17) | copy-start | bytes 1382404
  556.3 1.6 copy-start.51
  557.6 276.5 %all-reduce.12.cloned.1.call-start = ((), (), s32[]{:S(2)}) async-start(), calls=%async_computation.17 | async-start | bytes 3276800 | tf_op jit(solution)/shard_map/psum | solution.py:323
  583.8 4.1 copy-start.21
  584.0 3.9 copy-start.2
  584.0 3.9 copy-start.36
  589.2 1.6 copy-start.11
  591.1 18.4 %collective-permute-start.1 = (bf16[512,640]{0,1:T(8,128)(2,1)S(1)}, bf16[512,640]{0,1:T(8,128)(2,1)S(1)}, u32[]{:S(2)}, u32[]{:S(2)}) collective-permute-start(bf16[512,640]{0,1:T(8,128)(2,1)S(1)} %convert_element_type.267), channel_id=1, source_target_pairs={{4,0},{8,4},{12,8},{16,12},{20,16},{24,20},{28,24},{5,1},{9,5},{13... | collective-permute-start | bytes 1966088 | tf_op jit(solution)/shard_map/while/body/eval_jaxpr/ppermute | solution.py:24
  609.9 18.1 %collective-permute-start.1 = (bf16[512,640]{0,1:T(8,128)(2,1)S(1)}, bf16[512,640]{0,1:T(8,128)(2,1)S(1)}, u32[]{:S(2)}, u32[]{:S(2)}) collective-permute-start(bf16[512,640]{0,1:T(8,128)(2,1)S(1)} %convert_element_type.267), channel_id=1, source_target_pairs={{4,0},{8,4},{12,8},{16,12},{20,16},{24,20},{28,24},{5,1},{9,5},{13... | collective-permute-start | bytes 1966088 | tf_op jit(solution)/shard_map/while/body/eval_jaxpr/ppermute | solution.py:24
  628.5 17.5 %collective-permute-start.1 = (bf16[512,640]{0,1:T(8,128)(2,1)S(1)}, bf16[512,640]{0,1:T(8,128)(2,1)S(1)}, u32[]{:S(2)}, u32[]{:S(2)}) collective-permute-start(bf16[512,640]{0,1:T(8,128)(2,1)S(1)} %convert_element_type.267), channel_id=1, source_target_pairs={{4,0},{8,4},{12,8},{16,12},{20,16},{24,20},{28,24},{5,1},{9,5},{13... | collective-permute-start | bytes 1966088 | tf_op jit(solution)/shard_map/while/body/eval_jaxpr/ppermute | solution.py:24
  646.4 16.6 %collective-permute-start.1 = (bf16[512,640]{0,1:T(8,128)(2,1)S(1)}, bf16[512,640]{0,1:T(8,128)(2,1)S(1)}, u32[]{:S(2)}, u32[]{:S(2)}) collective-permute-start(bf16[512,640]{0,1:T(8,128)(2,1)S(1)} %convert_element_type.267), channel_id=1, source_target_pairs={{4,0},{8,4},{12,8},{16,12},{20,16},{24,20},{28,24},{5,1},{9,5},{13... | collective-permute-start | bytes 1966088 | tf_op jit(solution)/shard_map/while/body/eval_jaxpr/ppermute | solution.py:24
  663.4 15.6 %collective-permute-start.1 = (bf16[512,640]{0,1:T(8,128)(2,1)S(1)}, bf16[512,640]{0,1:T(8,128)(2,1)S(1)}, u32[]{:S(2)}, u32[]{:S(2)}) collective-permute-start(bf16[512,640]{0,1:T(8,128)(2,1)S(1)} %convert_element_type.267), channel_id=1, source_target_pairs={{4,0},{8,4},{12,8},{16,12},{20,16},{24,20},{28,24},{5,1},{9,5},{13... | collective-permute-start | bytes 1966088 | tf_op jit(solution)/shard_map/while/body/eval_jaxpr/ppermute | solution.py:24
  679.5 14.7 %collective-permute-start.1 = (bf16[512,640]{0,1:T(8,128)(2,1)S(1)}, bf16[512,640]{0,1:T(8,128)(2,1)S(1)}, u32[]{:S(2)}, u32[]{:S(2)}) collective-permute-start(bf16[512,640]{0,1:T(8,128)(2,1)S(1)} %convert_element_type.267), channel_id=1, source_target_pairs={{4,0},{8,4},{12,8},{16,12},{20,16},{24,20},{28,24},{5,1},{9,5},{13... | collective-permute-start | bytes 1966088 | tf_op jit(solution)/shard_map/while/body/eval_jaxpr/ppermute | solution.py:24
  694.7 86.8 %collective-permute-start.1 = (bf16[512,640]{0,1:T(8,128)(2,1)S(1)}, bf16[512,640]{0,1:T(8,128)(2,1)S(1)}, u32[]{:S(2)}, u32[]{:S(2)}) collective-permute-start(bf16[512,640]{0,1:T(8,128)(2,1)S(1)} %convert_element_type.267), channel_id=1, source_target_pairs={{4,0},{8,4},{12,8},{16,12},{20,16},{24,20},{28,24},{5,1},{9,5},{13... | collective-permute-start | bytes 1966088 | tf_op jit(solution)/shard_map/while/body/eval_jaxpr/ppermute | solution.py:24
  783.3 2.9 copy-start.39
  786.7 47.5 %copy-start.15 = (bf16[512,240]{0,1:T(8,128)(2,1)S(1)}, bf16[512,240]{0,1:T(8,128)(2,1)}, u32[]{:S(2)}) copy-start(bf16[512,240]{0,1:T(8,128)(2,1)} %param.19) | copy-start | bytes 737284
  786.7 47.5 %copy-start.45 = (f32[240]{0:T(256)S(1)}, f32[240]{0:T(256)}, u32[]{:S(2)}) copy-start(f32[240]{0:T(256)} %param.20) | copy-start | bytes 2884
  788.0 114.5 %reduce-scatter.33.cloned.1.call-start = ((), (), s32[]{:S(2)}) async-start(), calls=%async_computation.20 | async-start | bytes 1105920
  838.9 1.7 copy-start.4
  838.9 1.7 copy-start.34
  838.9 129.8 %reduce-scatter.29.cloned.1.call-start = ((), (), s32[]{:S(2)}) async-start(), calls=%async_computation.18 | async-start | bytes 1105920 | tf_op jit(solution)/shard_map/reduce_scatter | solution.py:362
  840.5 201.4 %reduce-scatter.39.cloned.1.call-start = ((), (), s32[]{:S(2)}) async-start(), calls=%async_computation.23 | async-start | bytes 2764800
  843.1 272.1 %reduce-scatter.41.cloned.1.call-start = ((), (), s32[]{:S(2)}) async-start(), calls=%async_computation.24 | async-start | bytes 2764800
  846.6 341.5 %reduce-scatter.43.cloned.1.call-start = ((), (), s32[]{:S(2)}) async-start(), calls=%async_computation.25 | async-start | bytes 2764800
  850.3 2.4 copy-start.54
  850.3 3.9 copy-start.25
  850.3 401.9 %reduce-scatter.35.cloned.1.call-start = ((), (), s32[]{:S(2)}) async-start(), calls=%async_computation.21 | async-start | bytes 368640
  852.7 464.0 %reduce-scatter.37.cloned.1.call-start = ((), (), s32[]{:S(2)}) async-start(), calls=%async_computation.22 | async-start | bytes 368640
  854.2 8.4 copy-start.49
  854.2 47.1 %copy-start.46 = (f32[512]{0:T(512)S(1)}, f32[512]{0:T(512)}, u32[]{:S(2)}) copy-start(f32[512]{0:T(512)} %get-tuple-element.925) | copy-start | bytes 6148
  (19 other events, 23.0 us)
Sparse Core Ops, SparseCore 0:
  118.2 38.8 reduce-scatter.24
  312.9 39.7 all-gather.4
  355.2 42.4 all-gather.6
  399.9 40.2 all-gather.8
  442.5 40.2 all-gather.10
  490.7 34.3 all-reduce.9
  527.7 24.7 reduce-scatter.26
  557.8 24.8 reduce-scatter.30
  788.1 45.9 all-reduce.11
  839.0 63.4 reduce-scatter.32
  906.4 62.2 reduce-scatter.28
  973.2 68.6 reduce-scatter.38
  1046.5 68.5 reduce-scatter.40
  1119.6 68.4 reduce-scatter.42
  1192.1 60.0 reduce-scatter.34
  1256.3 60.3 reduce-scatter.36
where the time goes:
time: 1320 us
  waiting for transfers between devices  954 us (72%)
  blocking collectives  204 us (15%)
  starting transfers between devices  49.8 us (4%)
  matrix products  43.5 us (3%)
  local copies, waits for them, and re-layouts  35 us (3%)
  other arithmetic  20.4 us (2%)
  between operations  15.5 us (1%)
    unnamed x23, waiting for transfers between devices  374 us
    ppermute x14, waiting for transfers between devices, shifted(): lax.ppermute(value, axis, [(source, source + steps) for source in range(l...  261 us
    reduce_scatter x1, waiting for transfers between devices, on_device(): lax.psum_scatter(grad_out, 'tok', scatter_dimension=0, tiled=True)  64.6 us
    ppermute x14, starting transfers between devices, shifted(): lax.ppermute(value, axis, [(source, source + steps) for source in range(l...  48.6 us
    psum x1, waiting for transfers between devices, on_device(): lax.psum(jnp.concatenate([query_grad_block, key_gradient_block, gradient_...  46.1 us
    all_gather x1, waiting for transfers between devices, on_device(): lax.all_gather(w_gate, 'tok', axis=0, tiled=True)  41.5 us
    all_gather x1, waiting for transfers between devices, on_device(): lax.all_gather(w_up, 'tok', axis=0, tiled=True)  39.2 us
    all_gather x1, waiting for transfers between devices, on_device(): lax.all_gather(w_down, 'tok', axis=1, tiled=True)  39.1 us
  transfers between devices with their start and end apart: 30, of which 30 were waited for; matrix products, arithmetic and copies ran while one was open for 3% of the time, Pallas kernels for 0%

commit v1 on v0

v1 whole, which is shorter than its diff:
```python
import itertools
import math

import jax
import jax.numpy as jnp
from jax import lax
from jax.experimental import pallas as pl
from jax.experimental.pallas import tpu as pltpu
from jax.sharding import PartitionSpec as P

MODEL_WIDTH = 960
QUERY_HEADS = 15
KEY_HEADS = 5
HEAD_SIZE = 64
SEQ_LEN = 4096
QUERY_PER_KEY = 3


EPS = 1e-05
ROPE_BASE = 10000.0
LARGE_NEGATIVE = -1e30


def rotary_tables(positions):
    half_width = HEAD_SIZE // 2
    inverse_freq = ROPE_BASE ** (-2.0 * jnp.arange(half_width, dtype=jnp.float32) / HEAD_SIZE)
    angles = positions.astype(jnp.float32)[:, None] * inverse_freq[None, :]
    return (jnp.cos(angles)[:, None, :], jnp.sin(angles)[:, None, :])


def apply_rotary(value_matrix, cosine_lookup, sine_lookup, head_count, sign_value):
    shaped = value_matrix.reshape(value_matrix.shape[0], head_count, HEAD_SIZE)
    lead_half = shaped[..., : HEAD_SIZE // 2]
    tail_half = shaped[..., HEAD_SIZE // 2 :]
    out_lead = lead_half * cosine_lookup - sign_value * tail_half * sine_lookup
    out_tail = tail_half * cosine_lookup + sign_value * lead_half * sine_lookup
    return jnp.concatenate([out_lead, out_tail], axis=-1).reshape(
        value_matrix.shape[0], head_count * HEAD_SIZE
    )


def divide_pair(value_matrix):
    high = value_matrix.astype(jnp.bfloat16)
    high = lax.optimization_barrier(high)
    low = (value_matrix - high.astype(jnp.float32)).astype(jnp.bfloat16)
    return high.astype(jnp.float32) + low.astype(jnp.float32)


VMEM_LIMIT = 56 * 1024 * 1024


class Place:
    def __init__(self, span):
        self.tok = lax.axis_index("tok")
        self.feat = lax.axis_index("feat")
        self.span = span
        tok_count, feat_count = lax.axis_size("tok"), lax.axis_size("feat")
        self.sizes = {"k": tok_count // 2, "ks": span // 2, "y": 2, "x": feat_count // 2, "c": 2}
        within = lax.rem(self.tok, span)
        self.base = self.tok - within
        self.at = {
            "k": lax.div(self.tok, 2),
            "ks": lax.div(within, 2),
            "y": lax.rem(self.tok, 2),
            "x": lax.div(self.feat, 2),
            "c": lax.rem(self.feat, 2),
        }

    def moved(self, dim, step):
        return lax.rem(self.at[dim] + step, self.sizes[dim])

    def index(self, offsets):
        result = 0
        for dim in ("k", "ks", "y", "x", "c"):
            if dim in offsets:
                result = result * self.sizes[dim] + self.moved(dim, offsets[dim])
        return result

    def peer(self, dim, step):
        tok, feat = self.tok, self.feat
        value = self.moved(dim, step)
        if dim == "k":
            tok = value * 2 + self.at["y"]
        elif dim == "ks":
            tok = self.base + value * 2 + self.at["y"]
        elif dim == "y":
            tok = self.at["k"] * 2 + value
        elif dim == "x":
            feat = value * 2 + self.at["c"]
        else:
            feat = self.at["x"] * 2 + value
        return {"tok": tok, "feat": feat}


def greet(place, dims):
    barrier = pltpu.get_barrier_semaphore()
    count = 0
    for dim in dims:
        for step in range(1, place.sizes[dim]):
            pl.semaphore_signal(
                barrier,
                inc=1,
                device_id=place.peer(dim, step),
                device_id_type=pl.DeviceIdType.MESH,
            )
            count += 1
    pl.semaphore_wait(barrier, count)


def all_dims(jobs):
    return [dim for dim in ("k", "ks", "y", "x", "c") if any(dim in job for job in jobs)]


def dim_sizes(span):
    return {
        "k": lax.axis_size("tok") // 2,
        "ks": span // 2,
        "y": 2,
        "x": lax.axis_size("feat") // 2,
        "c": 2,
    }


def staged_gather(arrays, jobs, collective, span):
    sizes = dim_sizes(span)
    count = len(arrays)
    slots = {}
    for j, dims in enumerate(jobs):
        for s, dim in enumerate(dims):
            for held in itertools.product(*[range(sizes[d]) for d in dims[:s]]):
                for step in range(1, sizes[dim]):
                    slots[j, s, held, step] = len(slots)
    totals = [math.prod(sizes[d] for d in dims) for dims in jobs]

    def kernel(*refs):
        ins, outs = refs[:count], refs[count : 2 * count]
        send_sem, recv_sem, local_sem = refs[2 * count :]
        place = Place(span)
        greet(place, all_dims(jobs))

        def block(j, held):
            dims = jobs[j]
            offsets = dict(zip(dims, tuple(held) + (0,) * (len(dims) - len(held))))
            return outs[j].at[place.index(offsets)]

        def copy(j, s, held, step, src, dst):
            slot = slots[j, s, held, step]
            return pltpu.make_async_remote_copy(
                src_ref=src,
                dst_ref=dst,
                send_sem=send_sem.at[slot],
                recv_sem=recv_sem.at[slot],
                device_id=place.peer(jobs[j][s], step),
                device_id_type=pl.DeviceIdType.MESH,
            )

        sent = []

        def forward(j, held, first, src):
            dims = jobs[j]
            for s in range(first, len(dims)):
                padded = held + (0,) * (s - len(held))
                for step in range(1, sizes[dims[s]]):
                    moving = copy(j, s, padded, step, src, block(j, padded))
                    moving.start()
                    sent.append(moving)

        local = []
        for j in range(count):
            forward(j, (), 0, ins[j])
            own = pltpu.make_async_copy(ins[j], block(j, ()), local_sem.at[j])
            own.start()
            local.append(own)
        for s in range(max(len(dims) for dims in jobs)):
            for j, dims in enumerate(jobs):
                if s >= len(dims):
                    continue
                size = sizes[dims[s]]
                for held in itertools.product(*[range(sizes[d]) for d in dims[:s]]):
                    for step in range(1, size):
                        arrived = held + ((size - step) % size,)
                        landed = block(j, arrived)
                        copy(j, s, held, step, landed, landed).wait_recv()
                        forward(j, arrived, s + 1, landed)
        for moving in sent:
            moving.wait_send()
        for own in local:
            own.wait()

    return pl.pallas_call(
        kernel,
        out_shape=[
            jax.ShapeDtypeStruct((total,) + a.shape, a.dtype) for total, a in zip(totals, arrays)
        ],
        in_specs=[pl.BlockSpec(memory_space=pl.ANY)] * count,
        out_specs=[pl.BlockSpec(memory_space=pl.ANY)] * count,
        scratch_shapes=[
            pltpu.SemaphoreType.DMA((len(slots),)),
            pltpu.SemaphoreType.DMA((len(slots),)),
            pltpu.SemaphoreType.DMA((count,)),
        ],
        compiler_params=pltpu.CompilerParams(collective_id=collective, has_side_effects=True),
    )(*arrays)


def staged_reduce(arrays, jobs, collective, span):
    sizes = dim_sizes(span)
    count = len(arrays)
    slots, scratch, where = {}, [], {}
    for j, dims in enumerate(jobs):
        tile = arrays[j].shape[1:]
        for s in range(len(dims)):
            rest = math.prod(sizes[d] for d in dims[s + 1 :])
            for step in range(1, sizes[dims[s]]):
                for held in itertools.product(*[range(sizes[d]) for d in dims[s + 1 :]]):
                    slots[j, s, step, held] = len(slots)
            where["recv", j, s] = len(scratch)
            scratch.append(pltpu.VMEM(((sizes[dims[s]] - 1) * rest,) + tile, jnp.bfloat16))
            if s < len(dims) - 1:
                where["sum", j, s] = len(scratch)
                scratch.append(pltpu.VMEM((rest,) + tile, jnp.bfloat16))

    def flat(dims, held):
        result = 0
        for d, offset in zip(dims, held):
            result = result * sizes[d] + offset
        return result

    def kernel(*refs):
        ins, outs = refs[:count], refs[count : 2 * count]
        buffers = refs[2 * count : 2 * count + len(scratch)]
        send_sem, recv_sem = refs[2 * count + len(scratch) :]
        place = Place(span)
        greet(place, all_dims(jobs))

        def source(j, s, held):
            dims = jobs[j]
            if s == 0:
                return ins[j].at[place.index(dict(zip(dims, held)))]
            return buffers[where["sum", j, s - 1]].at[flat(dims[s:], held)]

        def landing(j, s, step, held):
            dims = jobs[j]
            rest = math.prod(sizes[d] for d in dims[s + 1 :])
            return buffers[where["recv", j, s]].at[(step - 1) * rest + flat(dims[s + 1 :], held)]

        def copy(j, s, step, held):
            slot = slots[j, s, step, held]
            return pltpu.make_async_remote_copy(
                src_ref=source(j, s, (step,) + held),
                dst_ref=landing(j, s, step, held),
                send_sem=send_sem.at[slot],
                recv_sem=recv_sem.at[slot],
                device_id=place.peer(jobs[j][s], step),
                device_id_type=pl.DeviceIdType.MESH,
            )

        sent = []

        def start(j, s, step, held):
            moving = copy(j, s, step, held)
            moving.start()
            sent.append(moving)

        def offsets_of(dims):
            return reversed(list(itertools.product(*[range(sizes[d]) for d in dims])))

        for j, dims in enumerate(jobs):
            for held in offsets_of(dims[1:]):
                for step in range(1, sizes[dims[0]]):
                    start(j, 0, step, held)
        for s in range(max(len(dims) for dims in jobs)):
            for j, dims in enumerate(jobs):
                if s >= len(dims):
                    continue
                last = s == len(dims) - 1
                for held in offsets_of(dims[s + 1 :]):
                    steps = range(1, sizes[dims[s]])
                    for step in steps:
                        copy(j, s, step, held).wait_recv()
                    own = source(j, s, (0,) + held)
                    parts = [landing(j, s, step, held) for step in steps]
                    into = outs[j] if last else buffers[where["sum", j, s]].at[flat(dims[s + 1 :], held)]

                    @pl.loop(0, arrays[j].shape[1] // 16)
                    def _(chunk):
                        rows = pl.ds(pl.multiple_of(chunk * 16, 16), 16)
                        total = own[rows, :].astype(jnp.float32)
                        for part in parts:
                            total = total + part[rows, :].astype(jnp.float32)
                        into[rows, :] = total.astype(into.dtype)

                    if not last and held[0] != 0:
                        start(j, s + 1, held[0], held[1:])
        for moving in sent:
            moving.wait_send()

    return pl.pallas_call(
        kernel,
        out_shape=[jax.ShapeDtypeStruct(a.shape[1:], jnp.float32) for a in arrays],
        in_specs=[pl.BlockSpec(memory_space=pltpu.VMEM)] * count,
        out_specs=[pl.BlockSpec(memory_space=pltpu.VMEM)] * count,
        scratch_shapes=scratch
        + [pltpu.SemaphoreType.DMA((len(slots),)), pltpu.SemaphoreType.DMA((len(slots),))],
        compiler_params=pltpu.CompilerParams(
            collective_id=collective, has_side_effects=True, vmem_limit_bytes=VMEM_LIMIT
        ),
    )(*arrays)


def on_device(
    inputs, attn_gain, w_query, w_key, value_weight, w_out, ffn_gain, w_gate, w_up, w_down, cot
):
    f32, bf16 = jnp.float32, jnp.bfloat16
    token_rows, own_width = inputs.shape
    feat_count = lax.axis_size("feat")
    tok_count = lax.axis_size("tok")
    local_rows = token_rows // feat_count
    span = SEQ_LEN // token_rows
    query_width = QUERY_HEADS * HEAD_SIZE
    kv_width = KEY_HEADS * HEAD_SIZE
    qkv_width = query_width + 2 * kv_width
    score_scale = 1.0 / math.sqrt(HEAD_SIZE)
    feat_index = lax.axis_index("feat")
    depth = lax.rem(lax.axis_index("tok"), span)
    own_first = feat_index * local_rows
    rows = depth * token_rows + own_first + jnp.arange(local_rows, dtype=jnp.int32)
    cosine_lookup, sine_lookup = rotary_tables(rows)
    ff_own = w_gate.shape[1]
    out_rows = w_out.shape[0]
    padded_rows = -(-(out_rows + 1) // 16) * 16

    def padded(a):
        return jnp.pad(a, ((0, padded_rows - out_rows), (0, 0)))

    tok_dims, feat_dims = ("k", "y"), ("x", "c")
    qkv_shards, inputs_g, wo_shards, cot_g, gains_g, gate_up_shards, down_shards = staged_gather(
        [
            jnp.concatenate([w_query, w_key, value_weight], axis=1),
            inputs,
            padded(w_out),
            cot,
            jnp.broadcast_to(ffn_gain[None], (8, own_width)),
            padded(jnp.concatenate([w_gate, w_up], axis=1)),
            w_down,
        ],
        [tok_dims, feat_dims, tok_dims + feat_dims, feat_dims, feat_dims, tok_dims, tok_dims],
        0,
        span,
    )
    q_part, k_part = w_query.shape[1], w_key.shape[1]
    shard_columns = qkv_shards.transpose(1, 0, 2)
    qkv_weights = jnp.concatenate(
        [
            shard_columns[:, :, :q_part].reshape(own_width, query_width),
            shard_columns[:, :, q_part : q_part + k_part].reshape(own_width, kv_width),
            shard_columns[:, :, q_part + k_part :].reshape(own_width, kv_width),
        ],
        axis=1,
    )
    inputs_all = inputs_g.transpose(1, 0, 2).reshape(token_rows, MODEL_WIDTH)
    cot_all = cot_g.transpose(1, 0, 2).reshape(token_rows, MODEL_WIDTH)
    gain_all = gains_g[:, 0].reshape(MODEL_WIDTH)
    wo_all = (
        wo_shards.reshape(tok_count, feat_count, padded_rows, own_width)[:, :, :out_rows]
        .transpose(0, 2, 1, 3)
        .reshape(query_width, MODEL_WIDTH)
    )
    gate_up = gate_up_shards[:, :out_rows].reshape(MODEL_WIDTH, 2 * ff_own)
    wd_loc = down_shards.transpose(1, 0, 2).reshape(ff_own, MODEL_WIDTH)

    inputs_all_wide = inputs_all.astype(f32)
    inputs_wide = inputs.astype(f32)
    scale_one = lax.rsqrt(jnp.mean(inputs_all_wide * inputs_all_wide, axis=1, keepdims=True) + EPS)
    normed_one = (inputs_wide * scale_one * attn_gain[None, :]).astype(bf16)
    (projection,) = staged_reduce(
        [
            jnp.dot(normed_one, qkv_weights, preferred_element_type=f32)
            .astype(bf16)
            .reshape(feat_count, local_rows, qkv_width)
        ],
        [("c", "x")],
        1,
        span,
    )
    queries = apply_rotary(
        projection[:, :query_width], cosine_lookup, sine_lookup, QUERY_HEADS, 1.0
    ).astype(bf16)
    keys = apply_rotary(
        projection[:, query_width : query_width + kv_width],
        cosine_lookup,
        sine_lookup,
        KEY_HEADS,
        1.0,
    ).astype(bf16)
    values = projection[:, query_width + kv_width :].astype(bf16)
    (kv_shards,) = staged_gather(
        [jnp.concatenate([keys, values], axis=1)], [("ks", "y", "x", "c")], 2, span
    )
    kv_blocks = kv_shards.reshape(span, token_rows, 2 * kv_width)
    query_rows = queries.reshape(local_rows, KEY_HEADS, QUERY_PER_KEY, HEAD_SIZE).transpose(
        1, 2, 0, 3
    )

    def block_of(turn):
        piece = lax.dynamic_index_in_dim(kv_blocks, turn, 0, keepdims=False)
        return (
            piece[:, :kv_width].reshape(token_rows, KEY_HEADS, HEAD_SIZE),
            piece[:, kv_width:].reshape(token_rows, KEY_HEADS, HEAD_SIZE),
        )

    def allowed_of(turn):
        key_pos = turn * token_rows + jnp.arange(token_rows, dtype=jnp.int32)
        return key_pos[None, :] <= rows[:, None]

    def attend(turn, carried):
        maxima, totals, weighted = carried
        key_set, value_set = block_of(turn)
        scores = (
            jnp.einsum("gcrd,ngd->gcrn", query_rows, key_set, preferred_element_type=f32)
            * score_scale
        )
        masked = jnp.where(allowed_of(turn), scores, LARGE_NEGATIVE)
        new_max = jnp.maximum(maxima, jnp.max(masked, axis=-1))
        weights = jnp.exp(masked - new_max[..., None])
        factor = jnp.exp(maxima - new_max)
        return (
            new_max,
            totals * factor + jnp.sum(weights, axis=-1),
            weighted * factor[..., None]
            + jnp.einsum(
                "gcrn,ngd->gcrd", weights.astype(bf16), value_set, preferred_element_type=f32
            ),
        )

    state = (KEY_HEADS, QUERY_PER_KEY, local_rows)
    maxima, totals, weighted = lax.fori_loop(
        0,
        depth + 1,
        attend,
        (
            jnp.full(state, LARGE_NEGATIVE, f32),
            jnp.zeros(state, f32),
            jnp.zeros(state + (HEAD_SIZE,), f32),
        ),
    )
    heads_rows = (weighted / totals[..., None]).astype(bf16)
    heads_out = heads_rows.transpose(2, 0, 1, 3).reshape(local_rows, query_width)
    log_used = divide_pair(maxima + jnp.log(totals))
    (heads_g,) = staged_gather([heads_out], [feat_dims], 3, span)
    heads_all = heads_g.reshape(token_rows, query_width)

    residual_all = inputs_all_wide + jnp.dot(heads_all, wo_all, preferred_element_type=f32)
    scale_two = lax.rsqrt(jnp.mean(residual_all * residual_all, axis=1, keepdims=True) + EPS)
    normed_two = (residual_all * scale_two * gain_all[None, :]).astype(bf16)
    gate_up_pre = jnp.dot(normed_two, gate_up, preferred_element_type=f32)
    gate_pre, up_pre = gate_up_pre[:, :ff_own], gate_up_pre[:, ff_own:]
    sigmoid_gate = jax.nn.sigmoid(gate_pre)
    hidden = (gate_pre * sigmoid_gate * up_pre).astype(bf16)
    ffn_partial = jnp.dot(hidden, wd_loc, preferred_element_type=f32).astype(bf16)
    grad_down = jnp.dot(hidden.T, cot_all, preferred_element_type=f32)
    d_hidden = jnp.dot(cot_all, wd_loc.T, preferred_element_type=f32)
    d_gate = (d_hidden * up_pre * sigmoid_gate * (1.0 + gate_pre * (1.0 - sigmoid_gate))).astype(
        bf16
    )
    d_up = (d_hidden * gate_pre * sigmoid_gate).astype(bf16)
    d_gate_up = jnp.concatenate([d_gate, d_up], axis=1)
    grad_gate_up = jnp.dot(normed_two.T, d_gate_up, preferred_element_type=f32)
    back_two = jnp.dot(d_gate_up, gate_up.T, preferred_element_type=f32).astype(bf16)
    d_norm_two, ffn_term = staged_reduce(
        [
            back_two.reshape(feat_count, local_rows, MODEL_WIDTH),
            ffn_partial.reshape(token_rows, feat_count, own_width).transpose(1, 0, 2),
        ],
        [("c", "x"), ("c", "x")],
        4,
        span,
    )
    residual_own = lax.dynamic_slice_in_dim(
        residual_all, feat_index * own_width, own_width, 1
    )
    block_out = residual_own + ffn_term

    def own_rows(a):
        return lax.dynamic_slice_in_dim(a, own_first, local_rows, 0)

    residual_rows, scale_rows = own_rows(residual_all), own_rows(scale_two)
    stat_two = jnp.sum(d_norm_two * gain_all[None, :] * residual_rows, axis=1, keepdims=True)
    d_mid_rows = (
        own_rows(cot_all).astype(f32)
        + scale_rows * gain_all[None, :] * d_norm_two
        - residual_rows * scale_rows**3 * stat_two / MODEL_WIDTH
    ).astype(bf16)
    gain_two_rows = jnp.sum(d_norm_two * residual_rows * scale_rows, axis=0)
    head_gradient = (
        jnp.dot(d_mid_rows, wo_all.T, preferred_element_type=f32)
        .astype(bf16)
        .reshape(local_rows, KEY_HEADS, QUERY_PER_KEY, HEAD_SIZE)
        .transpose(1, 2, 0, 3)
    )
    delta_used = divide_pair(
        jnp.sum(head_gradient.astype(f32) * heads_rows.astype(f32), axis=-1)
    )

    def backprop(turn, carried):
        query_sum, gradients = carried
        key_set, value_set = block_of(turn)
        scores = (
            jnp.einsum("gcrd,ngd->gcrn", query_rows, key_set, preferred_element_type=f32)
            * score_scale
        )
        masked = jnp.where(allowed_of(turn), scores, LARGE_NEGATIVE)
        probability = jnp.exp(masked - log_used[..., None])
        d_probs = jnp.einsum(
            "gcrd,ngd->gcrn", head_gradient, value_set, preferred_element_type=f32
        )
        d_scores = (probability * (d_probs - delta_used[..., None])).astype(bf16)
        query_sum = (
            query_sum
            + jnp.einsum("gcrn,ngd->gcrd", d_scores, key_set, preferred_element_type=f32)
            * score_scale
        )
        key_part = (
            jnp.einsum("gcrn,gcrd->ngd", d_scores, query_rows, preferred_element_type=f32)
            * score_scale
        )
        value_part = jnp.einsum(
            "gcrn,gcrd->ngd",
            probability.astype(bf16),
            head_gradient,
            preferred_element_type=f32,
        )
        part = jnp.concatenate(
            [key_part.reshape(token_rows, kv_width), value_part.reshape(token_rows, kv_width)],
            axis=1,
        ).astype(bf16)
        return (query_sum, lax.dynamic_update_index_in_dim(gradients, part, turn, 0))

    query_sum, gradients = lax.fori_loop(
        0,
        depth + 1,
        backprop,
        (
            jnp.zeros(state + (HEAD_SIZE,), f32),
            jnp.zeros((span, token_rows, 2 * kv_width), bf16),
        ),
    )
    (kv_gradient,) = staged_reduce(
        [gradients.reshape(span * feat_count, local_rows, 2 * kv_width)],
        [("c", "x", "y", "ks")],
        5,
        span,
    )
    d_qkv_rows = jnp.concatenate(
        [
            apply_rotary(
                query_sum.transpose(2, 0, 1, 3).reshape(local_rows, query_width),
                cosine_lookup,
                sine_lookup,
                QUERY_HEADS,
                -1.0,
            ),
            apply_rotary(
                kv_gradient[:, :kv_width], cosine_lookup, sine_lookup, KEY_HEADS, -1.0
            ),
            kv_gradient[:, kv_width:],
        ],
        axis=1,
    ).astype(bf16)
    d_qkv_g, d_mid_g, gain_two_g = staged_gather(
        [d_qkv_rows, d_mid_rows, jnp.broadcast_to(gain_two_rows[None], (8, MODEL_WIDTH))],
        [feat_dims, feat_dims, feat_dims],
        6,
        span,
    )
    d_qkv_all = d_qkv_g.reshape(token_rows, qkv_width)
    d_mid_all = d_mid_g.reshape(token_rows, MODEL_WIDTH)
    d_attn = lax.dynamic_slice_in_dim(d_mid_all, feat_index * own_width, own_width, 1)
    gain_two_term = lax.dynamic_slice_in_dim(
        jnp.sum(gain_two_g[:, 0], axis=0), feat_index * own_width, own_width, 0
    )
    grad_out = jnp.dot(heads_all.T, d_attn, preferred_element_type=f32)
    projection_gradient = jnp.dot(normed_one.T, d_qkv_all, preferred_element_type=f32)
    back_one = jnp.dot(d_qkv_all, qkv_weights.T, preferred_element_type=f32)
    stat_own = jnp.sum(back_one * attn_gain[None, :] * inputs_wide, axis=1)
    (stat_g,) = staged_gather(
        [jnp.broadcast_to(stat_own[None], (8, token_rows))], [feat_dims], 7, span
    )
    stat_one = jnp.sum(stat_g[:, 0], axis=0)[:, None]
    grad_inputs = (
        d_attn.astype(f32)
        + scale_one * attn_gain[None, :] * back_one
        - inputs_wide * scale_one**3 * stat_one / MODEL_WIDTH
    )
    gain_one_term = jnp.sum(back_one * inputs_wide * scale_one, axis=0)

    def split_columns(a):
        return a.reshape(a.shape[0], tok_count, -1)

    qkv_term = jnp.concatenate(
        [
            split_columns(projection_gradient[:, :query_width]),
            split_columns(projection_gradient[:, query_width : query_width + kv_width]),
            split_columns(projection_gradient[:, query_width + kv_width :]),
        ],
        axis=2,
    ).transpose(1, 0, 2)
    down_term = split_columns(grad_down).transpose(1, 0, 2)
    rows_term = jnp.concatenate([grad_out, grad_gate_up], axis=1)
    rows_width = rows_term.shape[1]
    gains_row = jnp.pad(
        jnp.concatenate([gain_one_term, gain_two_term]), (0, rows_width - 2 * own_width)
    )
    rows_term = jnp.concatenate(
        [
            rows_term.reshape(tok_count, out_rows, rows_width),
            jnp.broadcast_to(gains_row[None, None], (tok_count, 1, rows_width)),
            jnp.zeros((tok_count, padded_rows - out_rows - 1, rows_width), f32),
        ],
        axis=1,
    )
    rows_sum, down_sum, qkv_sum = staged_reduce(
        [rows_term.astype(bf16), down_term.astype(bf16), qkv_term.astype(bf16)],
        [("y", "k")] * 3,
        8,
        span,
    )
    return (
        block_out.T,
        grad_inputs.T,
        rows_sum[out_rows, :own_width],
        qkv_sum[:, :q_part],
        qkv_sum[:, q_part : q_part + k_part],
        qkv_sum[:, q_part + k_part :],
        rows_sum[:out_rows, :own_width],
        rows_sum[out_rows, own_width : 2 * own_width],
        rows_sum[:out_rows, own_width : own_width + ff_own],
        rows_sum[:out_rows, own_width + ff_own :],
        down_sum,
    )


def solution(mesh):
    return jax.shard_map(
        on_device,
        mesh=mesh,
        in_specs=(
            P("tok", "feat"),
            P("feat"),
            P("feat", "tok"),
            P("feat", "tok"),
            P("feat", "tok"),
            P("tok", "feat"),
            P("feat"),
            P("tok", "feat"),
            P("tok", "feat"),
            P("feat", "tok"),
            P("tok", "feat"),
        ),
        out_specs=(
            P("feat", "tok"),
            P("feat", "tok"),
            P("feat"),
            P("feat", "tok"),
            P("feat", "tok"),
            P("feat", "tok"),
            P("tok", "feat"),
            P("feat"),
            P("tok", "feat"),
            P("tok", "feat"),
            P("feat", "tok"),
        ),
        check_vma=False,
    )
```

time: 1320 us -> 587 us (0.44)
  waiting for transfers between devices: 954 us -> 0 us
  Pallas kernels: 0 us -> 440 us
  blocking collectives: 204 us -> 0 us
  starting transfers between devices: 49.8 us -> 0 us
  local copies, waits for them, and re-layouts: 35 us -> 81.6 us
  between operations: 15.5 us -> 1.41 us
    pallas_call x0 -> x9, Pallas kernels: none -> 440 us  [the longest x4 273 us: staged_reduce(): pl.pallas_call(kernel, out_shape=[jax.ShapeDtypeStruct(a.shape[1:], jnp.f...]
    unnamed x23 -> x0, waiting for transfers between devices: 374 us -> none
    ppermute x14 -> x0, waiting for transfers between devices: 261 us -> none  [shifted(): lax.ppermute(value, axis, [(source, source + steps) for source in range(l...]
    all_gather x7 -> x0, blocking collectives: 151 us -> none  [the longest x1 31.8 us: on_device(): lax.all_gather(w_query, 'tok', axis=1, tiled=True)]
    all_gather x4 -> x0, waiting for transfers between devices: 147 us -> none  [the longest x1 41.5 us: on_device(): lax.all_gather(w_gate, 'tok', axis=0, tiled=True)]
    reduce_scatter x3 -> x0, waiting for transfers between devices: 94.9 us -> none  [the longest x1 64.6 us: on_device(): lax.psum_scatter(grad_out, 'tok', scatter_dimension=0, tiled=True)]
    psum x2 -> x0, waiting for transfers between devices: 77.3 us -> none  [the longest x1 46.1 us: on_device(): lax.psum(jnp.concatenate([query_grad_block, key_gradient_block, gradient_...]
    ppermute x14 -> x0, starting transfers between devices: 48.6 us -> none  [shifted(): lax.ppermute(value, axis, [(source, source + steps) for source in range(l...]
  transfers between devices with their start and end apart: 30 -> 0, of which waited for: 30 -> 0; matrix products, arithmetic and copies ran while one was open for 3% -> 0% of each run, Pallas kernels for 0% -> 0%
where the time goes in v1:
time: 587 us; the launch traced here: 585 us
  Pallas kernels  440 us (75%)
  local copies, waits for them, and re-layouts  81.6 us (14%)
  matrix products  41.9 us (7%)
  other arithmetic  20.2 us (3%)
    pallas_call x4, Pallas kernels, staged_reduce(): pl.pallas_call(kernel, out_shape=[jax.ShapeDtypeStruct(a.shape[1:], jnp.f...  273 us
    pallas_call x5, Pallas kernels, staged_gather(): pl.pallas_call(kernel, out_shape=[jax.ShapeDtypeStruct((total,) + a.shape...  166 us
    unnamed x72, local copies, waits for them, and re-layouts  24.3 us

profile of v1, /device:TPU:0, one launch (start us, length us, event | category | flops | bytes accessed | tf_op | source)
XLA Modules:
  0.0 585.1 jit_solution(3965872764744839650)
XLA Ops:
  2.4 1.6 pad_maximum_fusion.11.refs_0_
  4.0 1.8 copy.100.refs_1_
  5.8 1.5 pad.12.refs_2_
  7.2 1.8 copy.101.refs_3_
  9.0 1.3 broadcast_in_dim.40.refs_4_
  10.3 1.7 fusion.47.refs_5_
  12.8 80.1 %shard_map.194 = (bf16[8,240,200]{2,1,0:T(8,128)(2,1)}, bf16[4,512,240]{2,1,0:T(8,128)(2,1)}, bf16[32,128,240]{2,1,0:T(8,128)(2,1)}, bf16[4,512,240]{2,1,0:T(8,1...) custom-call(bf16[240,200]{1,0:T(8,128)(2,1)} %pad_maximum_fusion.11.refs_0_, ...), custom_call_target="tpu_custom_call" | custom-call | tf_op jit(solution)/shard_map/pallas_call | solution.py:190
  92.9 3.5 slice.131
  96.6 1.8 copy.103
  98.4 2.9 copy.114
  102.2 1.0 copy.104
  104.1 1.7 convolution_convert_fusion.1
  105.9 2.4 copy.107
  108.3 16.9 %shard_map.195 = f32[128,1600]{1,0:T(8,128)} custom-call(bf16[4,128,1600]{2,1,0:T(8,128)(2,1)} %bitcast.238), custom_call_target="tpu_custom_call" | custom-call | tf_op jit(solution)/shard_map/pallas_call | solution.py:298
  126.2 1.1 slice.122
  128.5 45.9 %shard_map.196 = bf16[32,128,640]{2,1,0:T(8,128)(2,1)} custom-call(bf16[128,640]{1,0:T(8,128)(2,1)} %pad_maximum_fusion.10.refs_0_), custom_call_target="tpu_custom_call" | custom-call | tf_op jit(solution)/shard_map/pallas_call | solution.py:190
  174.4 7.9 %copy.111 = bf16[8,512,640]{1,2,0:T(8,128)(2,1)} copy(bf16[8,512,640]{2,1,0:T(8,128)(2,1)} %bitcast.231) | data formatting | bytes 10485760
  182.7 4.3 while.28
  182.9 1.1 dynamic-slice_bitcast_fusion.4
  185.7 1.1 fusion.126
  187.9 10.5 %shard_map.197 = bf16[4,128,960]{2,1,0:T(8,128)(2,1)} custom-call(bf16[128,960]{1,0:T(8,128)(2,1)} %copy.112.refs_0_), custom_call_target="tpu_custom_call" | custom-call | tf_op jit(solution)/shard_map/pallas_call | solution.py:190
  198.4 1.7 slice.169
  200.1 2.5 copy.151
  202.6 3.4 reshape.296
  206.0 4.5 multiply_reduce_fusion
  211.4 5.4 fusion.59
  216.8 2.2 copy.116
  219.0 2.4 copy.117
  221.4 4.8 multiply_convert_fusion.3
  227.3 2.5 convolution_convert_fusion.5
  229.7 2.3 copy.118
  232.0 3.4 convolution_convert_fusion.4
  235.4 2.3 copy.119
  237.7 18.6 %shard_map.198 = (f32[128,960]{1,0:T(8,128)}, f32[512,240]{1,0:T(8,128)}) custom-call(bf16[4,128,960]{2,1,0:T(8,128)(2,1)} %bitcast.240, bf16[4,512,240]{2,1,0:T(8,128)(2,1)} %bitcast.241), custom_call_target="tpu_custom_call" | custom-call | tf_op jit(solution)/shard_map/pallas_call | solution.py:298
  256.3 2.4 add_bitcast_fusion
  258.6 2.0 copy.134
  260.7 1.0 constant_dynamic-slice_fusion.1
  262.5 1.2 multiply_reduce_fusion.1
  263.8 1.4 subtract_convert_fusion.refs_1_
  266.3 2.7 broadcast_in_dim.43.clone
  269.0 11.1 %while.29 = (s32[]{:T(128)}, f32[5,3,128,64]{2,3,1,0:T(8,128)S(1)}, bf16[8,512,640]{2,1,0:T(8,128)(2,1)}, s32[]{:T(128)}, bf16[8,512,640]{1,2,0:T(8,128)(2,1)}, ...) while((s32[]{:T(128)}, f32[5,3,128,64]{2,3,1,0:T(8,128)S(1)}, ...), condition=%wide.region_9.10_spmd.clone, body=%wide.region_8.9_spmd.clone.sunk | while | flops 641090176 | bytes 43806436 | solution.py:539
  269.0 1.1 dynamic-slice_bitcast_fusion.5
  270.2 2.6 fusion.138
  272.9 3.6 fusion.139
  277.0 1.1 fusion.141
  280.4 158.5 %shard_map.199 = f32[128,640]{1,0:T(8,128)} custom-call(bf16[32,128,640]{2,1,0:T(8,128)(2,1)} %bitcast.230), custom_call_target="tpu_custom_call" | custom-call | tf_op jit(solution)/shard_map/pallas_call | solution.py:298
  439.0 1.0 slice.136
  440.3 1.0 slice.206
  442.9 24.4 %shard_map.200 = (bf16[4,128,1600]{2,1,0:T(8,128)(2,1)}, bf16[4,128,960]{2,1,0:T(8,128)(2,1)}, f32[4,8,960]{2,1,0:T(8,128)}) custom-call(bf16[128,1600]{1,0:T(8,128)(2,1)} %concatenate.74.refs_0_, bf16[128,960]{1,0:T(8,128)(2,1)} %copy-done.3, f32[8,960]{1,0:T(8,128)} %broadcast_in_dim.44.refs_2_), custom_call_target="tpu_custom_call" | custom-call | tf_op jit(solution)/shard_map/pallas_call | solution.py:190
  467.4 2.3 fusion.45
  469.7 1.3 constant_dynamic-slice_fusion
  471.7 5.3 shard_map.201
  480.0 2.9 convolution_convert_fusion
  483.4 1.4 pad_maximum_fusion.1
  484.9 2.5 maximum_maximum_fusion.refs_0_
  487.4 2.0 convolution_convert_fusion.3
  489.4 2.5 copy.127
  494.0 1.6 maximum_bitcast_fusion.refs_2_
  495.6 79.3 %shard_map.202 = (f32[128,1520]{1,0:T(8,128)}, f32[640,120]{1,0:T(8,128)}, f32[240,200]{1,0:T(8,128)}) custom-call(bf16[8,128,1520]{2,1,0:T(8,128)(2,1)} %maximum_maximum_fusion.refs_0_, bf16[8,640,120]{2,1,0:T(8,128)(2,1)} %bitcast.239, bf16[8,240,200]{2,1,0:T(8,128)(2,1)} %maximum_bitcast_fusion.refs_2_), custom_call_target="tpu_custom_call" | custom-call | tf_op jit(solution)/shard_map/pallas_call | solution.py:298
  575.0 1.4 fusion.65
  576.4 1.6 slice.146
  577.9 1.1 fusion.66
  580.5 1.6 slice.149
  582.0 2.1 fusion.64
  (150 shorter events, 27.0 us)
Async XLA Ops:
  0.6 11.4 %copy-start.18 = (bf16[640,120]{0,1:T(8,128)(2,1)S(1)}, bf16[640,120]{0,1:T(8,128)(2,1)}, u32[]{:S(2)}) copy-start(bf16[640,120]{0,1:T(8,128)(2,1)} %param.24) | copy-start | bytes 460804
  92.9 3.5 copy-start.1
  98.4 3.0 copy-start.6
  101.7 2.4 copy-start.4
  101.7 2.4 copy-start.22
  101.9 3.9 copy-start.14
  102.1 3.7 copy-start.16
  104.1 4.1 copy-start.19
  174.4 7.9 %slice-start = ((f32[128,1600]{1,0:T(8,128)}), f32[128,960]{1,0:T(8,128)S(1)}, s32[]{:S(2)}) async-start(f32[128,1600]{1,0:T(8,128)} %shard_map.195), calls=%async_computation | async-start | bytes 1048576 | tf_op jit(solution)/shard_map/slice | solution.py:387
  211.4 51.1 %copy-start.25 = (f32[512]{0:T(512)}, f32[512]{0:T(512)S(1)}, u32[]{:S(2)}) copy-start(f32[512]{0:T(512)S(1)} %add_rsqrt_fusion) | copy-start | bytes 6148
  221.4 5.8 copy-start.2
  226.2 0.8 copy-start.28
  226.2 1.0 copy-start.29
  256.3 6.3 %copy-start.7 = (f32[128,960]{1,0:T(8,128)S(1)}, f32[128,960]{1,0:T(8,128)}, u32[]{:S(2)}) copy-start(f32[128,960]{1,0:T(8,128)} %get-tuple-element.136) | copy-start | bytes 1474564
  265.1 3.9 copy-start.3
  272.9 4.1 copy-start
  438.9 28.4 %copy-start.5 = (bf16[512,240]{0,1:T(8,128)(2,1)S(1)}, bf16[512,240]{0,1:T(8,128)(2,1)}, u32[]{:S(2)}) copy-start(bf16[512,240]{0,1:T(8,128)(2,1)} %param.15) | copy-start | bytes 737284
  438.9 28.4 %copy-start.12 = (bf16[240,8,120]{0,2,1:T(8,128)(2,1)S(1)}, bf16[240,8,120]{0,2,1:T(8,128)(2,1)}, u32[]{:S(2)}) copy-start(bf16[240,8,120]{0,2,1:T(8,128)(2,1)} %copy.104) | copy-start | bytes 1382404
  438.9 28.4 %copy-start.15 = (bf16[240,8,40]{0,2,1:T(8,128)(2,1)S(1)}, bf16[240,8,40]{0,2,1:T(8,128)(2,1)}, u32[]{:S(2)}) copy-start(bf16[240,8,40]{0,2,1:T(8,128)(2,1)} %copy-done.14) | copy-start | bytes 460804
  438.9 28.4 %copy-start.17 = (bf16[240,8,40]{0,2,1:T(8,128)(2,1)S(1)}, bf16[240,8,40]{0,2,1:T(8,128)(2,1)}, u32[]{:S(2)}) copy-start(bf16[240,8,40]{0,2,1:T(8,128)(2,1)} %copy-done.16) | copy-start | bytes 460804
  438.9 28.4 %copy-start.20 = (f32[512]{0:T(512)S(1)}, f32[512]{0:T(512)}, u32[]{:S(2)}) copy-start(f32[512]{0:T(512)} %copy-done.19) | copy-start | bytes 6148
  439.0 28.4 %copy-start.23 = (f32[240]{0:T(256)S(1)}, f32[240]{0:T(256)}, u32[]{:S(2)}) copy-start(f32[240]{0:T(256)} %param.16) | copy-start | bytes 2884
  467.3 10.6 %copy-start.21 = (f32[512]{0:T(512)S(1)}, f32[512]{0:T(512)}, u32[]{:S(2)}) copy-start(f32[512]{0:T(512)} %get-tuple-element.347) | copy-start | bytes 6148
  467.3 10.5 %copy-start.24 = (f32[240]{0:T(256)S(1)}, f32[240]{0:T(256)}, u32[]{:S(2)}) copy-start(f32[240]{0:T(256)} %param.16) | copy-start | bytes 2884
  469.6 10.3 %copy-start.10 = (f32[512,960]{1,0:T(8,128)S(1)}, f32[512,960]{1,0:T(8,128)}, u32[]{:S(2)}) copy-start(f32[512,960]{1,0:T(8,128)} %get-tuple-element.353) | copy-start | bytes 5898244
  469.7 10.3 %copy-start.26 = (f32[512]{0:T(512)S(1)}, f32[512]{0:T(512)}, u32[]{:S(2)}) copy-start(f32[512]{0:T(512)} %copy-done.25) | copy-start | bytes 6148
  480.0 3.0 copy-start.11
  484.9 2.5 copy-start.9
  484.9 2.5 copy-start.27
  489.4 2.5 copy-start.8
  574.9 9.2 %copy-start.13 = (f32[640,120]{1,0:T(8,128)S(1)}, f32[640,120]{1,0:T(8,128)}, u32[]{:S(2)}) copy-start(f32[640,120]{1,0:T(8,128)} %get-tuple-element.275) | copy-start | bytes 921604

commit v2 on v1

--- a/solution.py
+++ b/solution.py
@@ -308,6 +308,32 @@
     )(*arrays)
 
 
+def moved_along(value, axis, step):
+    count = lax.axis_size(axis)
+    return lax.ppermute(value, axis, [(i, (i + step) % count) for i in range(count)])
+
+
+def placed_along(parts, axis):
+    count = lax.axis_size(axis)
+    index = lax.axis_index(axis)
+    result = jnp.zeros((count,) + parts[0].shape, parts[0].dtype)
+    for step, part in enumerate(parts):
+        result = lax.dynamic_update_index_in_dim(
+            result, part, lax.rem(index + count - step, count), 0
+        )
+    return result
+
+
+def exchanged_along(blocks, axis):
+    count = lax.axis_size(axis)
+    index = lax.axis_index(axis)
+
+    def picked(step):
+        return lax.dynamic_index_in_dim(blocks, lax.rem(index + step, count), 0, keepdims=False)
+
+    return [picked(0)] + [moved_along(picked(step), axis, step) for step in range(1, count)]
+
+
 def on_device(
     inputs, attn_gain, w_query, w_key, value_weight, w_out, ffn_gain, w_gate, w_up, w_down, cot
 ):
@@ -328,23 +354,26 @@
     cosine_lookup, sine_lookup = rotary_tables(rows)
     ff_own = w_gate.shape[1]
     out_rows = w_out.shape[0]
-    padded_rows = -(-(out_rows + 1) // 16) * 16
+    padded_rows = -(-(out_rows + 2) // 16) * 16
 
     def padded(a):
         return jnp.pad(a, ((0, padded_rows - out_rows), (0, 0)))
 
     tok_dims, feat_dims = ("k", "y"), ("x", "c")
-    qkv_shards, inputs_g, wo_shards, cot_g, gains_g, gate_up_shards, down_shards = staged_gather(
+    ffn_shard = jnp.concatenate([w_gate, w_up, w_down.T], axis=1)
+    ffn_shards = [ffn_shard] + [
+        moved_along(ffn_shard, "tok", step) for step in range(1, tok_count)
+    ]
+    early = -(-5 * tok_count // 8) + 1
+    qkv_shards, inputs_g, wo_shards, cot_g, gains_g = staged_gather(
         [
             jnp.concatenate([w_query, w_key, value_weight], axis=1),
             inputs,
             padded(w_out),
             cot,
             jnp.broadcast_to(ffn_gain[None], (8, own_width)),
-            padded(jnp.concatenate([w_gate, w_up], axis=1)),
-            w_down,
-        ],
-        [tok_dims, feat_dims, tok_dims + feat_dims, feat_dims, feat_dims, tok_dims, tok_dims],
+        ],
+        [tok_dims, feat_dims, tok_dims + feat_dims, feat_dims, feat_dims],
         0,
         span,
     )
@@ -366,8 +395,6 @@
         .transpose(0, 2, 1, 3)
         .reshape(query_width, MODEL_WIDTH)
     )
-    gate_up = gate_up_shards[:, :out_rows].reshape(MODEL_WIDTH, 2 * ff_own)
-    wd_loc = down_shards.transpose(1, 0, 2).reshape(ff_own, MODEL_WIDTH)
 
     inputs_all_wide = inputs_all.astype(f32)
     inputs_wide = inputs.astype(f32)
@@ -394,10 +421,18 @@
         1.0,
     ).astype(bf16)
     values = projection[:, query_width + kv_width :].astype(bf16)
-    (kv_shards,) = staged_gather(
-        [jnp.concatenate([keys, values], axis=1)], [("ks", "y", "x", "c")], 2, span
-    )
-    kv_blocks = kv_shards.reshape(span, token_rows, 2 * kv_width)
+    kv_own = jnp.concatenate([keys, values], axis=1)
+    cut = min(-(-kv_width // 128) * 128, 2 * kv_width)
+    kv_first, kv_second = staged_gather(
+        [kv_own[:, :cut], kv_own[:, cut:]],
+        [("ks", "y", "x", "c"), ("ks", "x", "y", "c")],
+        2,
+        span,
+    )
+    kv_blocks = jnp.concatenate([kv_first, kv_second], axis=2).reshape(
+        span, token_rows, 2 * kv_width
+    )
+    kv_blocks, ffn_shards[:early] = lax.optimization_barrier((kv_blocks, ffn_shards[:early]))
     query_rows = queries.reshape(local_rows, KEY_HEADS, QUERY_PER_KEY, HEAD_SIZE).transpose(
         1, 2, 0, 3
     )
@@ -450,6 +485,8 @@
     (heads_g,) = staged_gather([heads_out], [feat_dims], 3, span)
     heads_all = heads_g.reshape(token_rows, query_width)
 
+    ffn_weights = placed_along(ffn_shards, "tok").reshape(MODEL_WIDTH, 3 * ff_own)
+    gate_up, down_turned = ffn_weights[:, : 2 * ff_own], ffn_weights[:, 2 * ff_own :]
     residual_all = inputs_all_wide + jnp.dot(heads_all, wo_all, preferred_element_type=f32)
     scale_two = lax.rsqrt(jnp.mean(residual_all * residual_all, axis=1, keepdims=True) + EPS)
     normed_two = (residual_all * scale_two * gain_all[None, :]).astype(bf16)
@@ -457,15 +494,21 @@
     gate_pre, up_pre = gate_up_pre[:, :ff_own], gate_up_pre[:, ff_own:]
     sigmoid_gate = jax.nn.sigmoid(gate_pre)
     hidden = (gate_pre * sigmoid_gate * up_pre).astype(bf16)
-    ffn_partial = jnp.dot(hidden, wd_loc, preferred_element_type=f32).astype(bf16)
-    grad_down = jnp.dot(hidden.T, cot_all, preferred_element_type=f32)
-    d_hidden = jnp.dot(cot_all, wd_loc.T, preferred_element_type=f32)
+    ffn_partial = jnp.dot(hidden, down_turned.T, preferred_element_type=f32).astype(bf16)
+    d_hidden = jnp.dot(cot_all, down_turned, preferred_element_type=f32)
     d_gate = (d_hidden * up_pre * sigmoid_gate * (1.0 + gate_pre * (1.0 - sigmoid_gate))).astype(
         bf16
     )
     d_up = (d_hidden * gate_pre * sigmoid_gate).astype(bf16)
     d_gate_up = jnp.concatenate([d_gate, d_up], axis=1)
-    grad_gate_up = jnp.dot(normed_two.T, d_gate_up, preferred_element_type=f32)
+    ffn_gradient = jnp.concatenate(
+        [
+            jnp.dot(normed_two.T, d_gate_up, preferred_element_type=f32).astype(bf16),
+            jnp.dot(cot_all.T, hidden, preferred_element_type=f32).astype(bf16),
+        ],
+        axis=1,
+    ).reshape(tok_count, out_rows, 3 * ff_own)
+    ffn_parts = exchanged_along(ffn_gradient, "tok")
     back_two = jnp.dot(d_gate_up, gate_up.T, preferred_element_type=f32).astype(bf16)
     d_norm_two, ffn_term = staged_reduce(
         [
@@ -545,11 +588,21 @@
             jnp.zeros((span, token_rows, 2 * kv_width), bf16),
         ),
     )
-    (kv_gradient,) = staged_reduce(
-        [gradients.reshape(span * feat_count, local_rows, 2 * kv_width)],
-        [("c", "x", "y", "ks")],
-        5,
-        span,
+    gradients, d_mid_rows, ffn_parts[:early] = lax.optimization_barrier(
+        (gradients, d_mid_rows, ffn_parts[:early])
+    )
+    d_mid_parts = exchanged_along(
+        d_mid_rows.reshape(local_rows, feat_count, own_width).transpose(1, 0, 2), "feat"
+    )
+    gradients = gradients.reshape(span * feat_count, local_rows, 2 * kv_width)
+    kv_gradient = jnp.concatenate(
+        staged_reduce(
+            [gradients[:, :, :cut], gradients[:, :, cut:]],
+            [("c", "x", "y", "ks"), ("c", "y", "x", "ks")],
+            5,
+            span,
+        ),
+        axis=1,
     )
     d_qkv_rows = jnp.concatenate(
         [
@@ -567,15 +620,18 @@
         ],
         axis=1,
     ).astype(bf16)
-    d_qkv_g, d_mid_g, gain_two_g = staged_gather(
-        [d_qkv_rows, d_mid_rows, jnp.broadcast_to(gain_two_rows[None], (8, MODEL_WIDTH))],
-        [feat_dims, feat_dims, feat_dims],
+    d_qkv_rows, d_mid_parts, ffn_parts[early:] = lax.optimization_barrier(
+        (d_qkv_rows, d_mid_parts, ffn_parts[early:])
+    )
+    d_qkv_g, gain_two_g = staged_gather(
+        [d_qkv_rows, jnp.broadcast_to(gain_two_rows[None], (8, MODEL_WIDTH))],
+        [feat_dims, feat_dims],
         6,
         span,
     )
     d_qkv_all = d_qkv_g.reshape(token_rows, qkv_width)
-    d_mid_all = d_mid_g.reshape(token_rows, MODEL_WIDTH)
-    d_attn = lax.dynamic_slice_in_dim(d_mid_all, feat_index * own_width, own_width, 1)
+    d_attn = placed_along(d_mid_parts, "feat")
+    d_attn = d_attn.reshape(token_rows, own_width)
     gain_two_term = lax.dynamic_slice_in_dim(
         jnp.sum(gain_two_g[:, 0], axis=0), feat_index * own_width, own_width, 0
     )
@@ -605,38 +661,35 @@
         ],
         axis=2,
     ).transpose(1, 0, 2)
-    down_term = split_columns(grad_down).transpose(1, 0, 2)
-    rows_term = jnp.concatenate([grad_out, grad_gate_up], axis=1)
-    rows_width = rows_term.shape[1]
-    gains_row = jnp.pad(
-        jnp.concatenate([gain_one_term, gain_two_term]), (0, rows_width - 2 * own_width)
-    )
     rows_term = jnp.concatenate(
         [
-            rows_term.reshape(tok_count, out_rows, rows_width),
-            jnp.broadcast_to(gains_row[None, None], (tok_count, 1, rows_width)),
-            jnp.zeros((tok_count, padded_rows - out_rows - 1, rows_width), f32),
+            grad_out.reshape(tok_count, out_rows, own_width),
+            jnp.broadcast_to(
+                jnp.stack([gain_one_term, gain_two_term])[None], (tok_count, 2, own_width)
+            ),
+            jnp.zeros((tok_count, padded_rows - out_rows - 2, own_width), f32),
         ],
         axis=1,
     )
-    rows_sum, down_sum, qkv_sum = staged_reduce(
-        [rows_term.astype(bf16), down_term.astype(bf16), qkv_term.astype(bf16)],
-        [("y", "k")] * 3,
+    rows_sum, qkv_sum = staged_reduce(
+        [rows_term.astype(bf16), qkv_term.astype(bf16)],
+        [("y", "k")] * 2,
         8,
         span,
     )
+    ffn_sum = sum(part.astype(f32) for part in ffn_parts)
     return (
         block_out.T,
         grad_inputs.T,
-        rows_sum[out_rows, :own_width],
+        rows_sum[out_rows],
         qkv_sum[:, :q_part],
         qkv_sum[:, q_part : q_part + k_part],
         qkv_sum[:, q_part + k_part :],
-        rows_sum[:out_rows, :own_width],
-        rows_sum[out_rows, own_width : 2 * own_width],
-        rows_sum[:out_rows, own_width : own_width + ff_own],
-        rows_sum[:out_rows, own_width + ff_own :],
-        down_sum,
+        rows_sum[:out_rows],
+        rows_sum[out_rows + 1],
+        ffn_sum[:, :ff_own],
+        ffn_sum[:, ff_own : 2 * ff_own],
+        ffn_sum[:, 2 * ff_own :].T,
     )
 
 

time: 587 us -> 556 us (0.947)
  Pallas kernels: 440 us -> 256 us
  starting transfers between devices: 0 us -> 100 us
  local copies, waits for them, and re-layouts: 81.6 us -> 120 us
  matrix products: 41.9 us -> 30.2 us
  loops' own time: 0.34 us -> 11.1 us
  other arithmetic: 20.2 us -> 29.7 us
    pallas_call x4, Pallas kernels: 273 us -> 102 us  [staged_reduce(): pl.pallas_call(kernel, out_shape=[jax.ShapeDtypeStruct(a.shape[1:], jnp.f...]
    ppermute x0 -> x17, starting transfers between devices: none -> 100 us  [moved_along(): lax.ppermute(value, axis, [(i, (i + step) % count) for i in range(count)])]
    dynamic_update_slice x2 -> x12, local copies, waits for them, and re-layouts: 1.19 us -> 23.9 us  [placed_along(): lax.dynamic_update_index_in_dim(result, part, lax.rem(index + count - ste...]
    pallas_call x5, Pallas kernels: 166 us -> 154 us  [staged_gather(): pl.pallas_call(kernel, out_shape=[jax.ShapeDtypeStruct((total,) + a.shape...]
    another operation x1, loops' own time: 0.07 us -> 10.7 us  [on_device(): lax.fori_loop(0, depth + 1, backprop, (jnp.zeros(state + (HEAD_SIZE,), f3...]
    optimization_barrier x0 -> x2, local copies, waits for them, and re-layouts: none -> 8.04 us  [on_device(): lax.optimization_barrier((gradients, d_mid_rows, ffn_parts[:early]))]
    unnamed x72 -> x74, local copies, waits for them, and re-layouts: 24.3 us -> 21.1 us
  transfers between devices with their start and end apart: 0 -> 17, of which waited for: 0 -> 0; matrix products, arithmetic and copies ran while one was open for 0% -> 21% of each run, Pallas kernels for 0% -> 35%
where the time goes in v2:
time: 556 us; the launch traced here: 549 us
  Pallas kernels  256 us (46%)
  local copies, waits for them, and re-layouts  120 us (22%)
  starting transfers between devices  100 us (18%)
  matrix products  30.2 us (5%)
  other arithmetic  29.7 us (5%)
  loops' own time  11.1 us (2%)
    pallas_call x5, Pallas kernels, staged_gather(): pl.pallas_call(kernel, out_shape=[jax.ShapeDtypeStruct((total,) + a.shape...  154 us
    pallas_call x4, Pallas kernels, staged_reduce(): pl.pallas_call(kernel, out_shape=[jax.ShapeDtypeStruct(a.shape[1:], jnp.f...  102 us
    ppermute x17, starting transfers between devices, moved_along(): lax.ppermute(value, axis, [(i, (i + step) % count) for i in range(count)])  100 us
    dynamic_update_slice x12, local copies, waits for them, and re-layouts, placed_along(): lax.dynamic_update_index_in_dim(result, part, lax.rem(index + count - ste...  23.9 us
    unnamed x74, local copies, waits for them, and re-layouts  21.1 us
  transfers between devices with their start and end apart: 17, of which 0 were waited for; matrix products, arithmetic and copies ran while one was open for 21% of the time, Pallas kernels for 35%

profile of v2, /device:TPU:0, one launch (start us, length us, event | category | flops | bytes accessed | tf_op | source)
XLA Modules:
  0.0 549.1 jit_solution(15604683270126803046)
XLA Ops:
  0.7 1.9 pad_maximum_fusion.6
  2.6 5.0 collective-permute-start.4
  7.9 1.6 collective-permute-start.2
  9.5 2.5 collective-permute-start.1
  12.0 1.5 collective-permute-start
  15.2 1.8 copy.53.refs_3_
  17.0 1.8 copy.52.refs_1_
  18.8 1.5 pad.4.refs_2_
  21.6 84.6 %shard_map.194 = (bf16[8,240,200]{2,1,0:T(8,128)(2,1)}, bf16[4,512,240]{2,1,0:T(8,128)(2,1)}, bf16[32,128,240]{2,1,0:T(8,128)(2,1)}, bf16[4,512,240]{2,1,0:T(8,128)(2,1)}, f32[4,8,240]{2,1,0:T(8,128)}) custom-call(bf16[240,200]{1,0:T(8,128)(2,1)} %pad_maximum_fusion.11.refs_0_, bf16[512,240]{1,0:T(8,128)(2,1)} %copy.52.refs_1_, ...), custom_call_target="tpu_custom_call" | custom-call | tf_op jit(solution)/shard_map/pallas_call | solution.py:190
  107.4 2.6 fusion.66
  114.7 2.9 convolution_convert_fusion.1
  117.6 3.6 copy.58
  121.2 16.5 %shard_map.195 = f32[128,1600]{1,0:T(8,128)} custom-call(bf16[4,128,1600]{2,1,0:T(8,128)(2,1)} %bitcast.286), custom_call_target="tpu_custom_call" | custom-call | tf_op jit(solution)/shard_map/pallas_call | solution.py:298
  140.7 3.0 slice.195
  143.7 4.2 copy.102
  147.9 4.4 reshape.301
  153.2 2.3 copy.67
  156.5 1.8 copy.54
  158.4 3.0 copy.65
  164.2 36.6 %shard_map.196 = (bf16[32,128,384]{2,1,0:T(8,128)(2,1)}, bf16[32,128,256]{2,1,0:T(8,128)(2,1)}) custom-call(bf16[128,384]{1,0:T(8,128)(2,1)} %pad_maximum_fusion.13.refs_0_, bf16[128,256]{1,0:T(8,128)(2,1)} %slice.192.refs_1_), custom_call_target="tpu_custom_call" | custom-call | tf_op jit(solution)/shard_map/pallas_call | solution.py:190
  200.8 5.8 %pad_maximum_fusion = bf16[32,128,640]{2,1,0:T(8,128)(2,1)} fusion(bf16[32,128,256]{2,1,0:T(8,128)(2,1)} %get-tuple-element.150, bf16[32,128,384]{2,1,0:T(8,128)(2,1)} %get-tuple-element.149), kind=kLoop, calls=%fused_computation.40 | loop fusion | flops 10485760 | bytes 10485760 | tf_op jit(solution)/shard_map/concatenate | solution.py:432
  206.6 4.7 collective-permute-start.6
  211.8 7.9 %copy.62 = bf16[8,512,640]{1,2,0:T(8,128)(2,1)} copy(bf16[8,512,640]{2,1,0:T(8,128)(2,1)} %bitcast.277) | data formatting | bytes 10485760
  219.7 4.4 while.28
  225.0 10.6 %shard_map.197 = bf16[4,128,960]{2,1,0:T(8,128)(2,1)} custom-call(bf16[128,960]{1,0:T(8,128)(2,1)} %copy.63.refs_0_), custom_call_target="tpu_custom_call" | custom-call | tf_op jit(solution)/shard_map/pallas_call | solution.py:190
  235.6 3.3 multiply_reduce_fusion
  239.3 1.4 bitcast_dynamic-update-slice_fusion.7
  248.2 1.6 fusion.35
  249.8 1.5 multiply_convert_fusion.3
  251.3 2.0 convolution_convert_fusion.3
  253.3 1.9 convolution_convert_fusion.4
  255.3 2.4 fusion.38
  257.7 3.0 convolution_convert_fusion
  260.7 2.3 copy.69
  263.0 2.3 copy.68
  265.3 18.7 %shard_map.198 = (f32[128,960]{1,0:T(8,128)}, f32[512,240]{1,0:T(8,128)}) custom-call(bf16[4,128,960]{2,1,0:T(8,128)(2,1)} %bitcast.290, bf16[4,512,240]{2,1,0:T(8,128)(2,1)} %bitcast.289), custom_call_target="tpu_custom_call" | custom-call | tf_op jit(solution)/shard_map/pallas_call | solution.py:298
  284.0 1.8 multiply_reduce_fusion.1
  285.8 1.4 subtract_convert_fusion
  288.6 1.9 dynamic-slice_bitcast_fusion.2
  290.5 20.5 %collective-permute-start.11 = (bf16[120,1920]{1,0:T(8,128)(2,1)}, bf16[120,1920]{1,0:T(8,128)(2,1)}, u32[]{:S(2)}, u32[]{:S(2)}) collective-permute-start(bf16[120,1920]{1,0:T(8,128)(2,1)} %get-tuple-element.345), channel_id=1, source_target_pairs={{0,20},{4,24},{8,28},{12,0},{16,4},{20,8},{24,12},{28,16},{1,21},{... | collective-permute-start | bytes 1382408 | tf_op jit(solution)/shard_map/ppermute | solution.py:313
  311.0 10.1 %collective-permute-start.9 = (bf16[120,1920]{1,0:T(8,128)(2,1)}, bf16[120,1920]{1,0:T(8,128)(2,1)}, u32[]{:S(2)}, u32[]{:S(2)}) collective-permute-start(bf16[120,1920]{1,0:T(8,128)(2,1)} %get-tuple-element.347), channel_id=1, source_target_pairs={{0,12},{4,16},{8,20},{12,24},{16,28},{20,0},{24,4},{28,8},{1,13},{... | collective-permute-start | bytes 1382408 | tf_op jit(solution)/shard_map/ppermute | solution.py:313
  321.2 4.4 collective-permute-start.7
  325.6 2.8 broadcast_in_dim.129
  328.5 17.4 %while.29 = (s32[]{:T(128)}, f32[5,3,128,64]{2,3,1,0:T(8,128)S(1)}, bf16[8,512,640]{1,2,0:T(8,128)(2,1)}, s32[]{:T(128)}, bf16[8,512,640]{1,2,0:T(8,128)(2,1)}, ...) while((s32[]{:T(128)}, f32[5,3,128,64]{2,3,1,0:T(8,128)S(1)}, ...), condition=%wide.region_9.10_spmd.clone, body=%wide.region_8.9_spmd.clone.sunk | while | flops 641090176 | bytes 25456332 | solution.py:582
  342.3 1.4 fusion.139
  345.8 2.2 add_bitcast_fusion
  348.5 2.0 copy.88
  350.8 47.3 %collective-permute-start.16 = (bf16[120,1920]{1,0:T(8,128)(2,1)}, bf16[120,1920]{1,0:T(8,128)(2,1)S(1)}, u32[]{:S(2)}, u32[]{:S(2)}) collective-permute-start(bf16[120,1920]{1,0:T(8,128)(2,1)} %get-tuple-element.343), channel_id=1, source_target_pairs={{0,28},{4,0},{8,4},{12,8},{16,12},{20,16},{24,20},{28,24},{1,29},{... | collective-permute-start | bytes 1382408 | tf_op jit(solution)/shard_map/ppermute | solution.py:313
  399.0 7.9 %copy.72 = bf16[8,512,640]{2,1,0:T(8,128)(2,1)} copy(bf16[8,512,640]{1,2,0:T(8,128)(2,1)} %get-tuple-element.168) | data formatting | bytes 10485760 | tf_op jit(solution)/shard_map/optimization_barrier | solution.py:591
  406.8 3.1 slice.203.refs_1_
  410.0 4.1 slice.202.refs_0_
  415.5 42.4 %shard_map.199 = (f32[128,384]{1,0:T(8,128)}, f32[128,256]{1,0:T(8,128)}) custom-call(bf16[32,128,384]{2,1,0:T(8,128)(2,1)} %slice.202.refs_0_, bf16[32,128,256]{2,1,0:T(8,128)(2,1)} %slice.203.refs_1_), custom_call_target="tpu_custom_call" | custom-call | tf_op jit(solution)/shard_map/pallas_call | solution.py:298
  462.9 16.8 %shard_map.200 = (bf16[4,128,1600]{2,1,0:T(8,128)(2,1)}, f32[4,8,960]{2,1,0:T(8,128)}) custom-call(bf16[128,1600]{1,0:T(8,128)(2,1)} %concatenate.80.refs_0_, f32[8,960]{1,0:T(8,128)} %broadcast_in_dim.134.refs_1_), custom_call_target="tpu_custom_call" | custom-call | tf_op jit(solution)/shard_map/pallas_call | solution.py:190
  479.7 3.1 fusion.52
  485.9 3.8 dynamic_update_slice.50
  489.6 3.8 dynamic_update_slice.51
  493.4 3.8 dynamic_update_slice.52
  497.1 3.8 dynamic_update_slice.53
  504.7 1.5 maximum_bitcast_fusion.refs_1_
  506.3 24.9 %shard_map.202 = (f32[128,240]{1,0:T(8,128)}, f32[240,200]{1,0:T(8,128)}) custom-call(bf16[8,128,240]{2,1,0:T(8,128)(2,1)} %maximum_maximum_fusion.refs_0_, bf16[8,240,200]{2,1,0:T(8,128)(2,1)} %maximum_bitcast_fusion.refs_1_), custom_call_target="tpu_custom_call" | custom-call | tf_op jit(solution)/shard_map/pallas_call | solution.py:298
  532.5 1.6 slice.173
  534.0 1.6 slice.170
  536.8 2.1 convert_add_fusion
  540.4 5.3 shard_map.201
  (211 shorter events, 58.7 us)
Async XLA Ops:
  0.6 19.6 %copy-start.22 = (bf16[240,120]{1,0:T(8,128)(2,1)S(1)}, bf16[240,120]{1,0:T(8,128)(2,1)}, u32[]{:S(2)}) copy-start(bf16[240,120]{1,0:T(8,128)(2,1)} %param.17) | copy-start | bytes 172804
  0.7 20.4 %copy-start.30 = (f32[240]{0:T(256)S(1)}, f32[240]{0:T(256)}, u32[]{:S(2)}) copy-start(f32[240]{0:T(256)} %param.21) | copy-start | bytes 2884
  2.6 204.0 %collective-permute-start.4 = (bf16[120,1920]{1,0:T(8,128)(2,1)}, bf16[120,1920]{1,0:T(8,128)(2,1)}, u32[]{:S(2)}, u32[]{:S(2)}) collective-permute-start(bf16[120,1920]{1,0:T(8,128)(2,1)} %pad_maximum_fusion.6), channel_id=1, source_target_pairs={{0,20},{4,24},{8,28},{12,0},{16,4},{20,8},{24,12},{28,16},{1,21},{... | collective-permute-start | bytes 1382408 | tf_op jit(solution)/shard_map/ppermute | solution.py:313
  7.6 203.7 %collective-permute-start.3 = (bf16[120,1920]{1,0:T(8,128)(2,1)}, bf16[120,1920]{1,0:T(8,128)(2,1)}, u32[]{:S(2)}, u32[]{:S(2)}) collective-permute-start(bf16[120,1920]{1,0:T(8,128)(2,1)} %pad_maximum_fusion.6), channel_id=1, source_target_pairs={{0,16},{4,20},{8,24},{12,28},{16,0},{20,4},{24,8},{28,12},{1,17},{... | collective-permute-start | bytes 1382408 | tf_op jit(solution)/shard_map/ppermute | solution.py:313
  7.9 203.9 %collective-permute-start.2 = (bf16[120,1920]{1,0:T(8,128)(2,1)}, bf16[120,1920]{1,0:T(8,128)(2,1)}, u32[]{:S(2)}, u32[]{:S(2)}) collective-permute-start(bf16[120,1920]{1,0:T(8,128)(2,1)} %pad_maximum_fusion.6), channel_id=1, source_target_pairs={{0,12},{4,16},{8,20},{12,24},{16,28},{20,0},{24,4},{28,8},{1,13},{... | collective-permute-start | bytes 1382408 | tf_op jit(solution)/shard_map/ppermute | solution.py:313
  9.5 202.3 %collective-permute-start.1 = (bf16[120,1920]{1,0:T(8,128)(2,1)}, bf16[120,1920]{1,0:T(8,128)(2,1)}, u32[]{:S(2)}, u32[]{:S(2)}) collective-permute-start(bf16[120,1920]{1,0:T(8,128)(2,1)} %pad_maximum_fusion.6), channel_id=1, source_target_pairs={{0,8},{4,12},{8,16},{12,20},{16,24},{20,28},{24,0},{28,4},{1,9},{5... | collective-permute-start | bytes 1382408 | tf_op jit(solution)/shard_map/ppermute | solution.py:313
  12.0 199.8 %collective-permute-start = (bf16[120,1920]{1,0:T(8,128)(2,1)}, bf16[120,1920]{1,0:T(8,128)(2,1)}, u32[]{:S(2)}, u32[]{:S(2)}) collective-permute-start(bf16[120,1920]{1,0:T(8,128)(2,1)} %pad_maximum_fusion.6), channel_id=1, source_target_pairs={{0,4},{4,8},{8,12},{12,16},{16,20},{20,24},{24,28},{28,0},{1,5},{5... | collective-permute-start | bytes 1382408 | tf_op jit(solution)/shard_map/ppermute | solution.py:313
  106.3 3.8 copy-start.1
  110.4 4.3 copy-start.4
  110.4 4.3 copy-start.28
  111.2 6.5 %copy-start.24 = (f32[512]{0:T(512)}, f32[512]{0:T(512)S(1)}, u32[]{:S(2)}) copy-start(f32[512]{0:T(512)S(1)} %get-tuple-element.376) | copy-start | bytes 6148
  113.4 7.8 %copy-start.19 = (bf16[240,8,40]{0,2,1:T(8,128)(2,1)}, bf16[240,8,40]{0,2,1:T(8,128)(2,1)S(1)}, u32[]{:S(2)}) copy-start(bf16[240,8,40]{0,2,1:T(8,128)(2,1)S(1)} %copy.56) | copy-start | bytes 460804
  114.6 6.5 %copy-start.20 = (bf16[240,8,40]{0,2,1:T(8,128)(2,1)}, bf16[240,8,40]{0,2,1:T(8,128)(2,1)S(1)}, u32[]{:S(2)}) copy-start(bf16[240,8,40]{0,2,1:T(8,128)(2,1)S(1)} %copy.57) | copy-start | bytes 460804
  139.9 3.8 copy-start.11
  153.2 130.8 %copy-start.23 = (f32[960]{0:T(1024)}, f32[960]{0:T(1024)S(1)}, u32[]{:S(2)}) copy-start(f32[960]{0:T(1024)S(1)} %mul.383) | copy-start | bytes 11524
  158.4 4.1 slice-start
  158.4 5.1 slice-start.1
  206.6 40.6 %collective-permute-start.6 = (bf16[120,1920]{1,0:T(8,128)(2,1)}, bf16[120,1920]{1,0:T(8,128)(2,1)}, u32[]{:S(2)}, u32[]{:S(2)}) collective-permute-start(bf16[120,1920]{1,0:T(8,128)(2,1)} %pad_maximum_fusion.6), channel_id=1, source_target_pairs={{0,28},{4,0},{8,4},{12,8},{16,12},{20,16},{24,20},{28,24},{1,29},{... | collective-permute-start | bytes 1382408 | tf_op jit(solution)/shard_map/ppermute | solution.py:313
  211.2 34.8 %collective-permute-start.5 = (bf16[120,1920]{1,0:T(8,128)(2,1)}, bf16[120,1920]{1,0:T(8,128)(2,1)}, u32[]{:S(2)}, u32[]{:S(2)}) collective-permute-start(bf16[120,1920]{1,0:T(8,128)(2,1)} %pad_maximum_fusion.6), channel_id=1, source_target_pairs={{0,24},{4,28},{8,0},{12,4},{16,8},{20,12},{24,16},{28,20},{1,25},{... | collective-permute-start | bytes 1382408 | tf_op jit(solution)/shard_map/ppermute | solution.py:313
  224.1 11.5 %copy-start = (bf16[960,960]{0,1:T(8,128)(2,1)S(1)}, bf16[960,960]{0,1:T(8,128)(2,1)}, u32[]{:S(2)}) copy-start(bf16[960,960]{0,1:T(8,128)(2,1)} %reshape.301) | copy-start | bytes 5529604
  238.9 18.8 %copy-start.9 = (f32[512,960]{1,0:T(8,128)}, f32[512,960]{1,0:T(8,128)S(1)}, u32[]{:S(2)}) copy-start(f32[512,960]{1,0:T(8,128)S(1)} %get-tuple-element.381) | copy-start | bytes 5898244
  248.2 1.6 copy-start.7
  265.3 18.7 %copy-start.10 = (f32[512,960]{1,0:T(8,128)S(1)}, f32[512,960]{1,0:T(8,128)}, u32[]{:S(2)}) copy-start(f32[512,960]{1,0:T(8,128)} %copy-done.9) | copy-start | bytes 5898244
  285.8 2.5 copy-start.3
  285.8 2.5 copy-start.8
  290.5 60.3 %collective-permute-start.11 = (bf16[120,1920]{1,0:T(8,128)(2,1)}, bf16[120,1920]{1,0:T(8,128)(2,1)}, u32[]{:S(2)}, u32[]{:S(2)}) collective-permute-start(bf16[120,1920]{1,0:T(8,128)(2,1)} %get-tuple-element.345), channel_id=1, source_target_pairs={{0,20},{4,24},{8,28},{12,0},{16,4},{20,8},{24,12},{28,16},{1,21},{... | collective-permute-start | bytes 1382408 | tf_op jit(solution)/shard_map/ppermute | solution.py:313
  311.0 87.0 %collective-permute-start.10 = (bf16[120,1920]{1,0:T(8,128)(2,1)}, bf16[120,1920]{1,0:T(8,128)(2,1)}, u32[]{:S(2)}, u32[]{:S(2)}) collective-permute-start(bf16[120,1920]{1,0:T(8,128)(2,1)} %get-tuple-element.346), channel_id=1, source_target_pairs={{0,16},{4,20},{8,24},{12,28},{16,0},{20,4},{24,8},{28,12},{1,17},{... | collective-permute-start | bytes 1382408 | tf_op jit(solution)/shard_map/ppermute | solution.py:313
  311.0 87.0 %collective-permute-start.9 = (bf16[120,1920]{1,0:T(8,128)(2,1)}, bf16[120,1920]{1,0:T(8,128)(2,1)}, u32[]{:S(2)}, u32[]{:S(2)}) collective-permute-start(bf16[120,1920]{1,0:T(8,128)(2,1)} %get-tuple-element.347), channel_id=1, source_target_pairs={{0,12},{4,16},{8,20},{12,24},{16,28},{20,0},{24,4},{28,8},{1,13},{... | collective-permute-start | bytes 1382408 | tf_op jit(solution)/shard_map/ppermute | solution.py:313
  321.2 76.9 %collective-permute-start.8 = (bf16[120,1920]{1,0:T(8,128)(2,1)}, bf16[120,1920]{1,0:T(8,128)(2,1)}, u32[]{:S(2)}, u32[]{:S(2)}) collective-permute-start(bf16[120,1920]{1,0:T(8,128)(2,1)} %get-tuple-element.348), channel_id=1, source_target_pairs={{0,8},{4,12},{8,16},{12,20},{16,24},{20,28},{24,0},{28,4},{1,9},{5... | collective-permute-start | bytes 1382408 | tf_op jit(solution)/shard_map/ppermute | solution.py:313
  321.2 76.9 %collective-permute-start.7 = (bf16[120,1920]{1,0:T(8,128)(2,1)}, bf16[120,1920]{1,0:T(8,128)(2,1)}, u32[]{:S(2)}, u32[]{:S(2)}) collective-permute-start(bf16[120,1920]{1,0:T(8,128)(2,1)} %get-tuple-element.349), channel_id=1, source_target_pairs={{0,4},{4,8},{8,12},{12,16},{16,20},{20,24},{24,28},{28,0},{1,5},{5... | collective-permute-start | bytes 1382408 | tf_op jit(solution)/shard_map/ppermute | solution.py:313
  328.4 17.4 %copy-start.12 = (f32[512,240]{1,0:T(8,128)S(1)}, f32[512,240]{1,0:T(8,128)}, u32[]{:S(2)}) copy-start(f32[512,240]{1,0:T(8,128)} %get-tuple-element.163) | copy-start | bytes 1474564
  328.4 19.5 %copy-start.2 = (bf16[4,128,960]{2,1,0:T(8,128)(2,1)S(1)}, bf16[4,128,960]{2,1,0:T(8,128)(2,1)}, u32[]{:S(2)}) copy-start(bf16[4,128,960]{2,1,0:T(8,128)(2,1)} %shard_map.197) | copy-start | bytes 2949124
  345.8 4.7 copy-start.21
  350.8 111.3 %collective-permute-start.16 = (bf16[120,1920]{1,0:T(8,128)(2,1)}, bf16[120,1920]{1,0:T(8,128)(2,1)S(1)}, u32[]{:S(2)}, u32[]{:S(2)}) collective-permute-start(bf16[120,1920]{1,0:T(8,128)(2,1)} %get-tuple-element.343), channel_id=1, source_target_pairs={{0,28},{4,0},{8,4},{12,8},{16,12},{20,16},{24,20},{28,24},{1,29},{... | collective-permute-start | bytes 1382408 | tf_op jit(solution)/shard_map/ppermute | solution.py:313
  398.1 64.0 %collective-permute-start.15 = (bf16[120,1920]{1,0:T(8,128)(2,1)}, bf16[120,1920]{1,0:T(8,128)(2,1)S(1)}, u32[]{:S(2)}, u32[]{:S(2)}) collective-permute-start(bf16[120,1920]{1,0:T(8,128)(2,1)} %get-tuple-element.344), channel_id=1, source_target_pairs={{0,24},{4,28},{8,0},{12,4},{16,8},{20,12},{24,16},{28,20},{1,25},{... | collective-permute-start | bytes 1382408 | tf_op jit(solution)/shard_map/ppermute | solution.py:313
  414.1 48.1 %collective-permute-start.14 = (bf16[128,240]{0,1:T(8,128)(2,1)}, bf16[128,240]{0,1:T(8,128)(2,1)S(1)}, u32[]{:S(2)}, u32[]{:S(2)}) collective-permute-start(bf16[128,240]{0,1:T(8,128)(2,1)} %get-tuple-element.365), channel_id=1, source_target_pairs={{0,3},{1,0},{2,1},{3,2},{4,7},{5,4},{6,5},{7,6},{8,11},{9,8},{10,9... | collective-permute-start | bytes 184328 | tf_op jit(solution)/shard_map/ppermute | solution.py:313
  414.1 48.1 %collective-permute-start.13 = (bf16[128,240]{0,1:T(8,128)(2,1)}, bf16[128,240]{0,1:T(8,128)(2,1)}, u32[]{:S(2)}, u32[]{:S(2)}) collective-permute-start(bf16[128,240]{0,1:T(8,128)(2,1)} %get-tuple-element.366), channel_id=1, source_target_pairs={{0,2},{1,3},{2,0},{3,1},{4,6},{5,7},{6,4},{7,5},{8,10},{9,11},{10,... | collective-permute-start | bytes 184328 | tf_op jit(solution)/shard_map/ppermute | solution.py:313
  415.3 46.8 %collective-permute-start.12 = (bf16[128,240]{0,1:T(8,128)(2,1)}, bf16[128,240]{0,1:T(8,128)(2,1)}, u32[]{:S(2)}, u32[]{:S(2)}) collective-permute-start(bf16[128,240]{0,1:T(8,128)(2,1)} %get-tuple-element.367), channel_id=1, source_target_pairs={{0,1},{1,2},{2,3},{3,0},{4,5},{5,6},{6,7},{7,4},{8,9},{9,10},{10,1... | collective-permute-start | bytes 184328 | tf_op jit(solution)/shard_map/ppermute | solution.py:313
  457.9 4.2 copy-start.26
  457.9 21.8 %copy-start.13 = (bf16[240,8,120]{0,2,1:T(8,128)(2,1)S(1)}, bf16[240,8,120]{0,2,1:T(8,128)(2,1)}, u32[]{:S(2)}) copy-start(bf16[240,8,120]{0,2,1:T(8,128)(2,1)} %copy.55) | copy-start | bytes 1382404
  457.9 21.8 %copy-start.25 = (f32[512]{0:T(512)S(1)}, f32[512]{0:T(512)}, u32[]{:S(2)}) copy-start(f32[512]{0:T(512)} %copy-done.24) | copy-start | bytes 6148
  457.9 21.8 %copy-start.29 = (f32[240]{0:T(256)S(1)}, f32[240]{0:T(256)}, u32[]{:S(2)}) copy-start(f32[240]{0:T(256)} %param.16) | copy-start | bytes 2884
  462.1 20.8 %copy-start.15 = (bf16[120,1920]{1,0:T(8,128)(2,1)}, bf16[120,1920]{1,0:T(8,128)(2,1)S(1)}, u32[]{:S(2)}) copy-start(bf16[120,1920]{1,0:T(8,128)(2,1)S(1)} %collective-permute-done.16) | copy-start | bytes 1382404
  462.1 20.7 %copy-start.17 = (bf16[120,1920]{1,0:T(8,128)(2,1)}, bf16[120,1920]{1,0:T(8,128)(2,1)S(1)}, u32[]{:S(2)}) copy-start(bf16[120,1920]{1,0:T(8,128)(2,1)S(1)} %collective-permute-done.15) | copy-start | bytes 1382404
  479.7 3.1 copy-start.6
  502.2 1.5 copy-start.31
  504.7 32.0 %copy-start.5 = (bf16[120,1920]{1,0:T(8,128)(2,1)S(1)}, bf16[120,1920]{1,0:T(8,128)(2,1)}, u32[]{:S(2)}) copy-start(bf16[120,1920]{1,0:T(8,128)(2,1)} %get-tuple-element.181) | copy-start | bytes 1382404
  504.7 32.0 %copy-start.16 = (bf16[120,1920]{1,0:T(8,128)(2,1)S(1)}, bf16[120,1920]{1,0:T(8,128)(2,1)}, u32[]{:S(2)}) copy-start(bf16[120,1920]{1,0:T(8,128)(2,1)} %copy-done.15) | copy-start | bytes 1382404
  504.7 32.1 %copy-start.18 = (bf16[120,1920]{1,0:T(8,128)(2,1)S(1)}, bf16[120,1920]{1,0:T(8,128)(2,1)}, u32[]{:S(2)}) copy-start(bf16[120,1920]{1,0:T(8,128)(2,1)} %copy-done.17) | copy-start | bytes 1382404
  536.8 11.2 %copy-start.14 = (f32[512,240]{0,1:T(8,128)S(1)}, f32[512,240]{0,1:T(8,128)}, u32[]{:S(2)}) copy-start(f32[512,240]{0,1:T(8,128)} %get-tuple-element.382) | copy-start | bytes 1474564
  536.8 11.2 %copy-start.27 = (f32[512]{0:T(512)S(1)}, f32[512]{0:T(512)}, u32[]{:S(2)}) copy-start(f32[512]{0:T(512)} %get-tuple-element.375) | copy-start | bytes 6148

commit v3 on v2

--- a/solution.py
+++ b/solution.py
@@ -360,11 +360,6 @@
         return jnp.pad(a, ((0, padded_rows - out_rows), (0, 0)))
 
     tok_dims, feat_dims = ("k", "y"), ("x", "c")
-    ffn_shard = jnp.concatenate([w_gate, w_up, w_down.T], axis=1)
-    ffn_shards = [ffn_shard] + [
-        moved_along(ffn_shard, "tok", step) for step in range(1, tok_count)
-    ]
-    early = -(-5 * tok_count // 8) + 1
     qkv_shards, inputs_g, wo_shards, cot_g, gains_g = staged_gather(
         [
             jnp.concatenate([w_query, w_key, value_weight], axis=1),
@@ -377,6 +372,12 @@
         0,
         span,
     )
+    ffn_shard = jnp.concatenate([w_gate, w_up, w_down.T], axis=1)
+    ffn_shard, qkv_shards = lax.optimization_barrier((ffn_shard, qkv_shards))
+    ffn_shards = [ffn_shard] + [
+        moved_along(ffn_shard, "tok", step) for step in range(1, tok_count)
+    ]
+    early = -(-5 * tok_count // 8) + 1
     q_part, k_part = w_query.shape[1], w_key.shape[1]
     shard_columns = qkv_shards.transpose(1, 0, 2)
     qkv_weights = jnp.concatenate(
@@ -588,12 +589,7 @@
             jnp.zeros((span, token_rows, 2 * kv_width), bf16),
         ),
     )
-    gradients, d_mid_rows, ffn_parts[:early] = lax.optimization_barrier(
-        (gradients, d_mid_rows, ffn_parts[:early])
-    )
-    d_mid_parts = exchanged_along(
-        d_mid_rows.reshape(local_rows, feat_count, own_width).transpose(1, 0, 2), "feat"
-    )
+    gradients, ffn_parts[:early] = lax.optimization_barrier((gradients, ffn_parts[:early]))
     gradients = gradients.reshape(span * feat_count, local_rows, 2 * kv_width)
     kv_gradient = jnp.concatenate(
         staged_reduce(
@@ -620,18 +616,17 @@
         ],
         axis=1,
     ).astype(bf16)
-    d_qkv_rows, d_mid_parts, ffn_parts[early:] = lax.optimization_barrier(
-        (d_qkv_rows, d_mid_parts, ffn_parts[early:])
-    )
-    d_qkv_g, gain_two_g = staged_gather(
-        [d_qkv_rows, jnp.broadcast_to(gain_two_rows[None], (8, MODEL_WIDTH))],
-        [feat_dims, feat_dims],
+    d_qkv_rows, ffn_parts[early:] = lax.optimization_barrier((d_qkv_rows, ffn_parts[early:]))
+    d_qkv_g, d_mid_g, gain_two_g = staged_gather(
+        [d_qkv_rows, d_mid_rows, jnp.broadcast_to(gain_two_rows[None], (8, MODEL_WIDTH))],
+        [feat_dims, feat_dims, feat_dims],
         6,
         span,
     )
     d_qkv_all = d_qkv_g.reshape(token_rows, qkv_width)
-    d_attn = placed_along(d_mid_parts, "feat")
-    d_attn = d_attn.reshape(token_rows, own_width)
+    d_attn = lax.dynamic_slice_in_dim(
+        d_mid_g.reshape(token_rows, MODEL_WIDTH), feat_index * own_width, own_width, 1
+    )
     gain_two_term = lax.dynamic_slice_in_dim(
         jnp.sum(gain_two_g[:, 0], axis=0), feat_index * own_width, own_width, 0
     )

time: 556 us -> 496 us (0.89)
  Pallas kernels: 256 us -> 221 us
  local copies, waits for them, and re-layouts: 120 us -> 108 us
  loops' own time: 11.1 us -> 0.32 us
    pallas_call x5, Pallas kernels: 154 us -> 107 us  [staged_gather(): pl.pallas_call(kernel, out_shape=[jax.ShapeDtypeStruct((total,) + a.shape...]
    dynamic_update_slice x12 -> x8, local copies, waits for them, and re-layouts: 23.9 us -> 8.87 us  [placed_along(): lax.dynamic_update_index_in_dim(result, part, lax.rem(index + count - ste...]
    pallas_call x4, Pallas kernels: 102 us -> 114 us  [staged_reduce(): pl.pallas_call(kernel, out_shape=[jax.ShapeDtypeStruct(a.shape[1:], jnp.f...]
    another operation x1, loops' own time: 10.7 us -> 0.05 us  [on_device(): lax.fori_loop(0, depth + 1, backprop, (jnp.zeros(state + (HEAD_SIZE,), f3...]
    unnamed x74 -> x87, local copies, waits for them, and re-layouts: 21.1 us -> 22 us
    ppermute x17 -> x14, starting transfers between devices: 100 us -> 99.8 us  [moved_along(): lax.ppermute(value, axis, [(i, (i + step) % count) for i in range(count)])]
  transfers between devices with their start and end apart: 17 -> 14, of which waited for: 0 -> 0; matrix products, arithmetic and copies ran while one was open for 21% -> 22% of each run, Pallas kernels for 35% -> 23%
where the time goes in v3:
time: 496 us; the launch traced here: 493 us
  Pallas kernels  221 us (45%)
  local copies, waits for them, and re-layouts  108 us (22%)
  starting transfers between devices  99.8 us (20%)
  other arithmetic  31.4 us (6%)
  matrix products  31.1 us (6%)
    pallas_call x4, Pallas kernels, staged_reduce(): pl.pallas_call(kernel, out_shape=[jax.ShapeDtypeStruct(a.shape[1:], jnp.f...  114 us
    pallas_call x5, Pallas kernels, staged_gather(): pl.pallas_call(kernel, out_shape=[jax.ShapeDtypeStruct((total,) + a.shape...  107 us
    ppermute x14, starting transfers between devices, moved_along(): lax.ppermute(value, axis, [(i, (i + step) % count) for i in range(count)])  99.8 us
    unnamed x87, local copies, waits for them, and re-layouts  22 us
  transfers between devices with their start and end apart: 14, of which 0 were waited for; matrix products, arithmetic and copies ran while one was open for 22% of the time, Pallas kernels for 23%

profile of v3, /device:TPU:0, one launch (start us, length us, event | category | flops | bytes accessed | tf_op | source)
XLA Modules:
  0.0 493.0 jit_solution(18361084280276378952)
XLA Ops:
  2.3 1.8 copy.54.refs_3_
  4.1 1.8 copy.53.refs_1_
  5.9 1.5 pad.4.refs_2_
  7.4 1.6 pad_maximum_fusion.11.refs_0_
  9.0 1.9 pad_maximum_fusion.6
  11.5 34.3 %shard_map.194 = (bf16[8,240,200]{2,1,0:T(8,128)(2,1)}, bf16[4,512,240]{2,1,0:T(8,128)(2,1)}, bf16[32,128,240]{2,1,0:T(8,128)(2,1)}, bf16[4,512,240]{2,1,0:T(8,128)(2,1)}, f32[4,8,240]{2,1,0:T(8,128)}) custom-call(bf16[240,200]{1,0:T(8,128)(2,1)} %pad_maximum_fusion.11.refs_0_, bf16[512,240]{1,0:T(8,128)(2,1)} %copy.53.refs_1_, ...), custom_call_target="tpu_custom_call" | custom-call | tf_op jit(solution)/shard_map/pallas_call | solution.py:190
  45.8 2.9 collective-permute-start.4
  49.5 2.5 collective-permute-start.2
  52.1 3.8 collective-permute-start.1
  56.9 1.8 slice.186
  58.7 2.6 fusion.67
  63.7 1.4 copy.57
  66.3 2.6 convolution_convert_fusion.1
  68.9 3.6 copy.59
  72.5 14.9 %shard_map.195 = f32[128,1600]{1,0:T(8,128)} custom-call(bf16[4,128,1600]{2,1,0:T(8,128)(2,1)} %bitcast.270), custom_call_target="tpu_custom_call" | custom-call | tf_op jit(solution)/shard_map/pallas_call | solution.py:298
  87.4 1.7 slice.141
  91.1 3.0 slice.195
  94.1 4.2 copy.99
  98.3 4.4 reshape.290
  104.2 1.5 copy.68
  106.5 1.8 copy.100
  108.2 1.8 copy.55
  110.1 3.0 copy.66
  115.8 33.4 %shard_map.196 = (bf16[32,128,384]{2,1,0:T(8,128)(2,1)}, bf16[32,128,256]{2,1,0:T(8,128)(2,1)}) custom-call(bf16[128,384]{1,0:T(8,128)(2,1)} %pad_maximum_fusion.13.refs_0_, bf16[128,256]{1,0:T(8,128)(2,1)} %slice.192.refs_1_), custom_call_target="tpu_custom_call" | custom-call | tf_op jit(solution)/shard_map/pallas_call | solution.py:190
  149.3 5.8 %pad_maximum_fusion = bf16[32,128,640]{2,1,0:T(8,128)(2,1)} fusion(bf16[32,128,256]{2,1,0:T(8,128)(2,1)} %get-tuple-element.149, bf16[32,128,384]{2,1,0:T(8,128)(2,1)} %get-tuple-element.148), kind=kLoop, calls=%fused_computation.40 | loop fusion | flops 10485760 | bytes 10485760 | tf_op jit(solution)/shard_map/concatenate | solution.py:433
  155.1 8.0 %collective-permute-start.6 = (bf16[120,1920]{1,0:T(8,128)(2,1)}, bf16[120,1920]{1,0:T(8,128)(2,1)}, u32[]{:S(2)}, u32[]{:S(2)}) collective-permute-start(bf16[120,1920]{1,0:T(8,128)(2,1)} %pad_maximum_fusion.6), channel_id=1, source_target_pairs={{0,28},{4,0},{8,4},{12,8},{16,12},{20,16},{24,20},{28,24},{1,29},{... | collective-permute-start | bytes 1382408 | tf_op jit(solution)/shard_map/ppermute | solution.py:313
  163.1 7.9 %copy.63 = bf16[8,512,640]{1,2,0:T(8,128)(2,1)} copy(bf16[8,512,640]{2,1,0:T(8,128)(2,1)} %bitcast.261) | data formatting | bytes 10485760
  171.0 4.3 while.28
  176.2 10.3 %shard_map.197 = bf16[4,128,960]{2,1,0:T(8,128)(2,1)} custom-call(bf16[128,960]{1,0:T(8,128)(2,1)} %copy.64.refs_0_), custom_call_target="tpu_custom_call" | custom-call | tf_op jit(solution)/shard_map/pallas_call | solution.py:190
  186.5 3.3 multiply_reduce_fusion
  190.2 1.4 bitcast_dynamic-update-slice_fusion.7
  199.1 1.6 fusion.35
  200.7 1.5 multiply_convert_fusion.3
  202.2 2.0 convolution_convert_fusion.3
  204.2 1.9 convolution_convert_fusion.4
  206.2 2.4 fusion.38
  208.6 3.1 convolution_convert_fusion
  211.7 2.3 copy.70
  213.9 2.3 copy.69
  216.2 18.8 %shard_map.198 = (f32[128,960]{1,0:T(8,128)}, f32[512,240]{1,0:T(8,128)}) custom-call(bf16[4,128,960]{2,1,0:T(8,128)(2,1)} %bitcast.274, bf16[4,512,240]{2,1,0:T(8,128)(2,1)} %bitcast.273), custom_call_target="tpu_custom_call" | custom-call | tf_op jit(solution)/shard_map/pallas_call | solution.py:298
  235.0 1.8 multiply_reduce_fusion.1
  236.8 1.4 subtract_convert_fusion.refs_1_
  239.9 1.9 dynamic-slice_bitcast_fusion.2
  241.8 19.2 %collective-permute-start.11 = (bf16[120,1920]{1,0:T(8,128)(2,1)}, bf16[120,1920]{1,0:T(8,128)(2,1)}, u32[]{:S(2)}, u32[]{:S(2)}) collective-permute-start(bf16[120,1920]{1,0:T(8,128)(2,1)} %get-tuple-element.341), channel_id=1, source_target_pairs={{0,20},{4,24},{8,28},{12,0},{16,4},{20,8},{24,12},{28,16},{1,21},{... | collective-permute-start | bytes 1382408 | tf_op jit(solution)/shard_map/ppermute | solution.py:313
  261.0 10.4 %collective-permute-start.9 = (bf16[120,1920]{1,0:T(8,128)(2,1)}, bf16[120,1920]{1,0:T(8,128)(2,1)}, u32[]{:S(2)}, u32[]{:S(2)}) collective-permute-start(bf16[120,1920]{1,0:T(8,128)(2,1)} %get-tuple-element.343), channel_id=1, source_target_pairs={{0,12},{4,16},{8,20},{12,24},{16,28},{20,0},{24,4},{28,8},{1,13},{... | collective-permute-start | bytes 1382408 | tf_op jit(solution)/shard_map/ppermute | solution.py:313
  271.4 4.4 collective-permute-start.7
  275.8 2.8 broadcast_in_dim.112
  278.7 6.7 %while.29 = (s32[]{:T(128)}, f32[5,3,128,64]{2,3,1,0:T(8,128)S(1)}, bf16[8,512,640]{1,2,0:T(8,128)(2,1)}, s32[]{:T(128)}, bf16[8,512,640]{1,2,0:T(8,128)(2,1)}, ...) while((s32[]{:T(128)}, f32[5,3,128,64]{2,3,1,0:T(8,128)S(1)}, ...), condition=%wide.region_9.10_spmd.clone, body=%wide.region_8.9_spmd.clone.sunk | while | flops 641090176 | bytes 25456332 | solution.py:583
  281.8 1.4 fusion.139
  285.5 1.4 add_bitcast_fusion
  286.9 47.3 %collective-permute-start.13 = (bf16[120,1920]{1,0:T(8,128)(2,1)}, bf16[120,1920]{1,0:T(8,128)(2,1)}, u32[]{:S(2)}, u32[]{:S(2)}) collective-permute-start(bf16[120,1920]{1,0:T(8,128)(2,1)} %get-tuple-element.339), channel_id=1, source_target_pairs={{0,28},{4,0},{8,4},{12,8},{16,12},{20,16},{24,20},{28,24},{1,29},{... | collective-permute-start | bytes 1382408 | tf_op jit(solution)/shard_map/ppermute | solution.py:313
  337.5 7.9 %copy.73 = bf16[8,512,640]{2,1,0:T(8,128)(2,1)} copy(bf16[8,512,640]{1,2,0:T(8,128)(2,1)} %get-tuple-element.168) | data formatting | bytes 10485760 | tf_op jit(solution)/shard_map/optimization_barrier | solution.py:592
  345.4 3.1 slice.203.refs_1_
  348.5 4.1 slice.202.refs_0_
  352.6 53.8 %shard_map.199 = (f32[128,384]{1,0:T(8,128)}, f32[128,256]{1,0:T(8,128)}) custom-call(bf16[32,128,384]{2,1,0:T(8,128)(2,1)} %slice.202.refs_0_, bf16[32,128,256]{2,1,0:T(8,128)(2,1)} %slice.203.refs_1_), custom_call_target="tpu_custom_call" | custom-call | tf_op jit(solution)/shard_map/pallas_call | solution.py:298
  411.2 23.9 %shard_map.200 = (bf16[4,128,1600]{2,1,0:T(8,128)(2,1)}, bf16[4,128,960]{2,1,0:T(8,128)(2,1)}, f32[4,8,960]{2,1,0:T(8,128)}) custom-call(bf16[128,1600]{1,0:T(8,128)(2,1)} %concatenate.80.refs_0_, bf16[128,960]{1,0:T(8,128)(2,1)} %copy-done.4, f32[8,960]{1,0:T(8,128)} %broadcast_in_dim.113.refs_2_), custom_call_target="tpu_custom_call" | custom-call | tf_op jit(solution)/shard_map/pallas_call | solution.py:190
  435.2 3.7 fusion.52
  447.1 1.6 maximum_bitcast_fusion.refs_1_
  448.7 26.2 %shard_map.202 = (f32[128,240]{1,0:T(8,128)}, f32[240,200]{1,0:T(8,128)}) custom-call(bf16[8,128,240]{2,1,0:T(8,128)(2,1)} %maximum_maximum_fusion.refs_0_, bf16[8,240,200]{2,1,0:T(8,128)(2,1)} %maximum_bitcast_fusion.refs_1_), custom_call_target="tpu_custom_call" | custom-call | tf_op jit(solution)/shard_map/pallas_call | solution.py:298
  474.9 1.3 fusion.70
  476.2 1.6 slice.173
  477.8 1.6 slice.170
  480.5 2.4 convert_add_fusion
  484.4 5.3 %shard_map.201 = f32[4,8,512]{2,1,0:T(8,128)} custom-call(f32[8,512]{1,0:T(8,128)} %broadcast_in_dim.114.refs_0_), custom_call_target="tpu_custom_call" | custom-call | tf_op jit(solution)/shard_map/pallas_call | solution.py:190
  (207 shorter events, 56.6 us)
Async XLA Ops:
  0.6 10.2 %copy-start.35 = (f32[240]{0:T(256)S(1)}, f32[240]{0:T(256)}, u32[]{:S(2)}) copy-start(f32[240]{0:T(256)} %param.21) | copy-start | bytes 2884
  45.8 15.6 %copy-start.1 = (bf16[4,512,240]{2,1,0:T(8,128)(2,1)S(1)}, bf16[4,512,240]{2,1,0:T(8,128)(2,1)}, u32[]{:S(2)}) copy-start(bf16[4,512,240]{2,1,0:T(8,128)(2,1)} %get-tuple-element.145) | copy-start | bytes 2949124
  45.8 109.3 %collective-permute-start.4 = (bf16[120,1920]{1,0:T(8,128)(2,1)}, bf16[120,1920]{1,0:T(8,128)(2,1)}, u32[]{:S(2)}, u32[]{:S(2)}) collective-permute-start(bf16[120,1920]{1,0:T(8,128)(2,1)} %pad_maximum_fusion.6), channel_id=1, source_target_pairs={{0,20},{4,24},{8,28},{12,0},{16,4},{20,8},{24,12},{28,16},{1,21},{... | collective-permute-start | bytes 1382408 | tf_op jit(solution)/shard_map/ppermute | solution.py:313
  48.7 114.4 %collective-permute-start.3 = (bf16[120,1920]{1,0:T(8,128)(2,1)}, bf16[120,1920]{1,0:T(8,128)(2,1)}, u32[]{:S(2)}, u32[]{:S(2)}) collective-permute-start(bf16[120,1920]{1,0:T(8,128)(2,1)} %pad_maximum_fusion.6), channel_id=1, source_target_pairs={{0,16},{4,20},{8,24},{12,28},{16,0},{20,4},{24,8},{28,12},{1,17},{... | collective-permute-start | bytes 1382408 | tf_op jit(solution)/shard_map/ppermute | solution.py:313
  49.5 113.5 %collective-permute-start.2 = (bf16[120,1920]{1,0:T(8,128)(2,1)}, bf16[120,1920]{1,0:T(8,128)(2,1)}, u32[]{:S(2)}, u32[]{:S(2)}) collective-permute-start(bf16[120,1920]{1,0:T(8,128)(2,1)} %pad_maximum_fusion.6), channel_id=1, source_target_pairs={{0,12},{4,16},{8,20},{12,24},{16,28},{20,0},{24,4},{28,8},{1,13},{... | collective-permute-start | bytes 1382408 | tf_op jit(solution)/shard_map/ppermute | solution.py:313
  52.1 111.0 %collective-permute-start.1 = (bf16[120,1920]{1,0:T(8,128)(2,1)}, bf16[120,1920]{1,0:T(8,128)(2,1)}, u32[]{:S(2)}, u32[]{:S(2)}) collective-permute-start(bf16[120,1920]{1,0:T(8,128)(2,1)} %pad_maximum_fusion.6), channel_id=1, source_target_pairs={{0,8},{4,12},{8,16},{12,20},{16,24},{20,28},{24,0},{28,4},{1,9},{5... | collective-permute-start | bytes 1382408 | tf_op jit(solution)/shard_map/ppermute | solution.py:313
  55.9 107.2 %collective-permute-start = (bf16[120,1920]{1,0:T(8,128)(2,1)}, bf16[120,1920]{1,0:T(8,128)(2,1)}, u32[]{:S(2)}, u32[]{:S(2)}) collective-permute-start(bf16[120,1920]{1,0:T(8,128)(2,1)} %pad_maximum_fusion.6), channel_id=1, source_target_pairs={{0,4},{4,8},{8,12},{12,16},{16,20},{20,24},{24,28},{28,0},{1,5},{5... | collective-permute-start | bytes 1382408 | tf_op jit(solution)/shard_map/ppermute | solution.py:313
  61.7 4.6 copy-start.5
  62.4 6.4 %copy-start.27 = (f32[512]{0:T(512)}, f32[512]{0:T(512)S(1)}, u32[]{:S(2)}) copy-start(f32[512]{0:T(512)S(1)} %get-tuple-element.368) | copy-start | bytes 6148
  63.7 5.2 %copy-start.20 = (bf16[240,8,120]{0,2,1:T(8,128)(2,1)}, bf16[240,8,120]{0,2,1:T(8,128)(2,1)S(1)}, u32[]{:S(2)}) copy-start(bf16[240,8,120]{0,2,1:T(8,128)(2,1)S(1)} %copy.56) | copy-start | bytes 1382404
  66.3 6.2 %copy-start.23 = (bf16[240,8,40]{0,2,1:T(8,128)(2,1)}, bf16[240,8,40]{0,2,1:T(8,128)(2,1)S(1)}, u32[]{:S(2)}) copy-start(bf16[240,8,40]{0,2,1:T(8,128)(2,1)S(1)} %copy.58) | copy-start | bytes 460804
  90.4 3.7 copy-start.17
  105.7 4.4 copy-start.9
  110.1 3.1 copy-start.18
  110.1 3.2 copy-start.37
  110.1 4.1 slice-start
  110.1 5.0 %slice-start.1 = ((bf16[128,1600]{1,0:T(8,128)(2,1)}), bf16[128,320]{1,0:T(8,128)(2,1)S(1)}, s32[]{:S(2)}) async-start(bf16[128,1600]{1,0:T(8,128)(2,1)} %copy-done.17), calls=%async_computation.1 | async-start | bytes 196608 | tf_op jit(solution)/shard_map/slice | solution.py:424
  155.1 42.9 %collective-permute-start.6 = (bf16[120,1920]{1,0:T(8,128)(2,1)}, bf16[120,1920]{1,0:T(8,128)(2,1)}, u32[]{:S(2)}, u32[]{:S(2)}) collective-permute-start(bf16[120,1920]{1,0:T(8,128)(2,1)} %pad_maximum_fusion.6), channel_id=1, source_target_pairs={{0,28},{4,0},{8,4},{12,8},{16,12},{20,16},{24,20},{28,24},{1,29},{... | collective-permute-start | bytes 1382408 | tf_op jit(solution)/shard_map/ppermute | solution.py:313
  163.0 33.9 %collective-permute-start.5 = (bf16[120,1920]{1,0:T(8,128)(2,1)}, bf16[120,1920]{1,0:T(8,128)(2,1)}, u32[]{:S(2)}, u32[]{:S(2)}) collective-permute-start(bf16[120,1920]{1,0:T(8,128)(2,1)} %pad_maximum_fusion.6), channel_id=1, source_target_pairs={{0,24},{4,28},{8,0},{12,4},{16,8},{20,12},{24,16},{28,20},{1,25},{... | collective-permute-start | bytes 1382408 | tf_op jit(solution)/shard_map/ppermute | solution.py:313
  175.3 11.2 %copy-start = (bf16[960,960]{0,1:T(8,128)(2,1)S(1)}, bf16[960,960]{0,1:T(8,128)(2,1)}, u32[]{:S(2)}) copy-start(bf16[960,960]{0,1:T(8,128)(2,1)} %reshape.290) | copy-start | bytes 5529604
  189.8 18.8 %copy-start.12 = (f32[512,960]{1,0:T(8,128)}, f32[512,960]{1,0:T(8,128)S(1)}, u32[]{:S(2)}) copy-start(f32[512,960]{1,0:T(8,128)S(1)} %get-tuple-element.373) | copy-start | bytes 5898244
  193.7 5.4 %copy-start.26 = (f32[960]{0:T(1024)S(1)}, f32[960]{0:T(1024)}, u32[]{:S(2)}) copy-start(f32[960]{0:T(1024)} %mul.384) | copy-start | bytes 11524
  199.1 1.6 copy-start.10
  216.2 18.8 %copy-start.13 = (f32[512,960]{1,0:T(8,128)S(1)}, f32[512,960]{1,0:T(8,128)}, u32[]{:S(2)}) copy-start(f32[512,960]{1,0:T(8,128)} %copy-done.12) | copy-start | bytes 5898244
  216.2 20.6 %copy-start.14 = (bf16[128,960]{1,0:T(8,128)(2,1)S(1)}, bf16[128,960]{1,0:T(8,128)(2,1)}, u32[]{:S(2)}) copy-start(bf16[128,960]{1,0:T(8,128)(2,1)} %copy.100) | copy-start | bytes 737284
  236.8 2.5 copy-start.3
  236.8 2.5 copy-start.11
  238.2 1.4 copy-start.4
  239.2 0.7 copy-start.15
  241.8 45.1 %collective-permute-start.11 = (bf16[120,1920]{1,0:T(8,128)(2,1)}, bf16[120,1920]{1,0:T(8,128)(2,1)}, u32[]{:S(2)}, u32[]{:S(2)}) collective-permute-start(bf16[120,1920]{1,0:T(8,128)(2,1)} %get-tuple-element.341), channel_id=1, source_target_pairs={{0,20},{4,24},{8,28},{12,0},{16,4},{20,8},{24,12},{28,16},{1,21},{... | collective-permute-start | bytes 1382408 | tf_op jit(solution)/shard_map/ppermute | solution.py:313
  261.0 73.2 %collective-permute-start.10 = (bf16[120,1920]{1,0:T(8,128)(2,1)}, bf16[120,1920]{1,0:T(8,128)(2,1)}, u32[]{:S(2)}, u32[]{:S(2)}) collective-permute-start(bf16[120,1920]{1,0:T(8,128)(2,1)} %get-tuple-element.342), channel_id=1, source_target_pairs={{0,16},{4,20},{8,24},{12,28},{16,0},{20,4},{24,8},{28,12},{1,17},{... | collective-permute-start | bytes 1382408 | tf_op jit(solution)/shard_map/ppermute | solution.py:313
  261.0 76.5 %collective-permute-start.9 = (bf16[120,1920]{1,0:T(8,128)(2,1)}, bf16[120,1920]{1,0:T(8,128)(2,1)}, u32[]{:S(2)}, u32[]{:S(2)}) collective-permute-start(bf16[120,1920]{1,0:T(8,128)(2,1)} %get-tuple-element.343), channel_id=1, source_target_pairs={{0,12},{4,16},{8,20},{12,24},{16,28},{20,0},{24,4},{28,8},{1,13},{... | collective-permute-start | bytes 1382408 | tf_op jit(solution)/shard_map/ppermute | solution.py:313
  271.4 66.1 %collective-permute-start.8 = (bf16[120,1920]{1,0:T(8,128)(2,1)}, bf16[120,1920]{1,0:T(8,128)(2,1)}, u32[]{:S(2)}, u32[]{:S(2)}) collective-permute-start(bf16[120,1920]{1,0:T(8,128)(2,1)} %get-tuple-element.344), channel_id=1, source_target_pairs={{0,8},{4,12},{8,16},{12,20},{16,24},{20,28},{24,0},{28,4},{1,9},{5... | collective-permute-start | bytes 1382408 | tf_op jit(solution)/shard_map/ppermute | solution.py:313
  271.4 66.1 %collective-permute-start.7 = (bf16[120,1920]{1,0:T(8,128)(2,1)}, bf16[120,1920]{1,0:T(8,128)(2,1)}, u32[]{:S(2)}, u32[]{:S(2)}) collective-permute-start(bf16[120,1920]{1,0:T(8,128)(2,1)} %get-tuple-element.345), channel_id=1, source_target_pairs={{0,4},{4,8},{8,12},{12,16},{16,20},{20,24},{24,28},{28,0},{1,5},{5... | collective-permute-start | bytes 1382408 | tf_op jit(solution)/shard_map/ppermute | solution.py:313
  275.8 2.9 copy-start.16
  278.7 6.7 %copy-start.25 = (f32[128,32]{0,1:T(8,128)S(1)}, f32[128,32]{0,1:T(8,128)}, u32[]{:S(2)}) copy-start(f32[128,32]{0,1:T(8,128)} %get-tuple-element.369) | copy-start | bytes 49156
  278.7 6.8 %copy-start.19 = (f32[512,240]{1,0:T(8,128)S(1)}, f32[512,240]{1,0:T(8,128)}, u32[]{:S(2)}) copy-start(f32[512,240]{1,0:T(8,128)} %get-tuple-element.163) | copy-start | bytes 1474564
  285.4 49.5 %copy-start.2 = (bf16[4,128,960]{2,1,0:T(8,128)(2,1)S(1)}, bf16[4,128,960]{2,1,0:T(8,128)(2,1)}, u32[]{:S(2)}) copy-start(bf16[4,128,960]{2,1,0:T(8,128)(2,1)} %shard_map.197) | copy-start | bytes 2949124
  286.9 123.7 %collective-permute-start.13 = (bf16[120,1920]{1,0:T(8,128)(2,1)}, bf16[120,1920]{1,0:T(8,128)(2,1)}, u32[]{:S(2)}, u32[]{:S(2)}) collective-permute-start(bf16[120,1920]{1,0:T(8,128)(2,1)} %get-tuple-element.339), channel_id=1, source_target_pairs={{0,28},{4,0},{8,4},{12,8},{16,12},{20,16},{24,20},{28,24},{1,29},{... | collective-permute-start | bytes 1382408 | tf_op jit(solution)/shard_map/ppermute | solution.py:313
  334.2 76.4 %collective-permute-start.12 = (bf16[120,1920]{1,0:T(8,128)(2,1)}, bf16[120,1920]{1,0:T(8,128)(2,1)}, u32[]{:S(2)}, u32[]{:S(2)}) collective-permute-start(bf16[120,1920]{1,0:T(8,128)(2,1)} %get-tuple-element.340), channel_id=1, source_target_pairs={{0,24},{4,28},{8,0},{12,4},{16,8},{20,12},{24,16},{28,20},{1,25},{... | collective-permute-start | bytes 1382408 | tf_op jit(solution)/shard_map/ppermute | solution.py:313
  406.4 4.2 copy-start.30
  406.4 28.7 %copy-start.21 = (bf16[240,8,120]{0,2,1:T(8,128)(2,1)S(1)}, bf16[240,8,120]{0,2,1:T(8,128)(2,1)}, u32[]{:S(2)}) copy-start(bf16[240,8,120]{0,2,1:T(8,128)(2,1)} %copy-done.20) | copy-start | bytes 1382404
  406.4 28.7 %copy-start.24 = (bf16[240,8,40]{0,2,1:T(8,128)(2,1)S(1)}, bf16[240,8,40]{0,2,1:T(8,128)(2,1)}, u32[]{:S(2)}) copy-start(bf16[240,8,40]{0,2,1:T(8,128)(2,1)} %copy-done.23) | copy-start | bytes 460804
  406.4 28.7 %copy-start.28 = (f32[512]{0:T(512)S(1)}, f32[512]{0:T(512)}, u32[]{:S(2)}) copy-start(f32[512]{0:T(512)} %copy-done.27) | copy-start | bytes 6148
  406.4 28.7 %copy-start.32 = (f32[240]{0:T(256)S(1)}, f32[240]{0:T(256)}, u32[]{:S(2)}) copy-start(f32[240]{0:T(256)} %param.16) | copy-start | bytes 2884
  435.2 3.7 copy-start.8
  441.7 4.5 copy-start.36
  442.9 3.3 copy-start.6
  447.1 33.4 %copy-start.7 = (bf16[120,1920]{1,0:T(8,128)(2,1)S(1)}, bf16[120,1920]{1,0:T(8,128)(2,1)}, u32[]{:S(2)}) copy-start(bf16[120,1920]{1,0:T(8,128)(2,1)} %get-tuple-element.177) | copy-start | bytes 1382404
  480.5 3.4 copy-start.34
  480.5 11.5 %copy-start.22 = (f32[512,240]{0,1:T(8,128)S(1)}, f32[512,240]{0,1:T(8,128)}, u32[]{:S(2)}) copy-start(f32[512,240]{0,1:T(8,128)} %get-tuple-element.374) | copy-start | bytes 1474564
  480.5 11.5 %copy-start.29 = (f32[512]{0:T(512)S(1)}, f32[512]{0:T(512)}, u32[]{:S(2)}) copy-start(f32[512]{0:T(512)} %copy-done.27) | copy-start | bytes 6148
  480.5 11.5 %copy-start.31 = (f32[512]{0:T(512)S(1)}, f32[512]{0:T(512)}, u32[]{:S(2)}) copy-start(f32[512]{0:T(512)} %get-tuple-element.367) | copy-start | bytes 6148
  480.5 11.5 %copy-start.33 = (f32[240]{0:T(256)S(1)}, f32[240]{0:T(256)}, u32[]{:S(2)}) copy-start(f32[240]{0:T(256)} %param.16) | copy-start | bytes 2884
